TPU v7x, 256 devices: a whole 4x4x8 slice. The times are simulated.
256 devices in a mesh: ctx: 64 (over x, z_lo, y), fsdp: 4 (over z_hi, core).
Axes of the slice: x: 4, y: 4, z: 8 (z_hi: 2, z_lo: 4; z = z_hi * 4 + z_lo), core: 2. Of those that a mesh axis runs over, the one named last changes fastest.
Arguments:
- inputs: bfloat16 [4, 16384, 4096], P('fsdp', 'ctx'), may hold values from -6 to 6
- gates: bfloat16 [4, 16384, 4096], P('fsdp', 'ctx'), may hold values from -6 to 6
- grad_out: bfloat16 [4, 16384, 4096], P('fsdp', 'ctx'), may hold values from -6 to 6
- doc_lengths: int32 [4, 64], P('fsdp'), may hold values from 1 to 1024, 16384 in all within a row
- short_filter: bfloat16 [7, 256], P(None, 'fsdp'), may hold values from -2 to 2
- long_filter: bfloat16 [128, 256], P(None, 'fsdp'), may hold values from -0.5 to 0.5
Outputs:
- grad_inputs: bfloat16 [4, 16384, 4096], P('fsdp', 'ctx')
- grad_gates: bfloat16 [4, 16384, 4096], P('fsdp', 'ctx')
- short_grad: float32 [7, 256], P(None, 'fsdp')
- long_grad: float32 [128, 256], P(None, 'fsdp')
Inputs may be any that keep to these rules, and one draw needn't show every extreme that they name: `doc_lengths`: each pack's 64 lengths sum to 16384, and one of them is exactly 1024.
All inputs are finite; a program needn't handle non-finite values.
Results may differ from a plain program's by a relative error of at most 0.012.
Values may be sent and summed in bfloat16 or wider, within the bound.
A program may use at most 128 MiB of HBM per device.

v0:
```python
import math

import jax
import jax.numpy as jnp
from jax import lax
from jax.sharding import PartitionSpec as P


def passed_along(block, axis, distance):
    devices = range(lax.axis_size(axis))
    route = [(i - distance, i) for i in devices if i - distance in devices]
    return lax.ppermute(block, axis, route)


def doc_starts(lengths, positions):
    doc_ends = jnp.cumsum(lengths)
    passed = (doc_ends[None, :] <= positions[:, None]).astype(jnp.int32)
    return jnp.sum(passed * lengths[None, :], axis=1)


def block_mask(lengths, source_pos, target_pos):
    return source_pos[:, None] >= doc_starts(lengths, target_pos)[None, :]


def channel_table(filters, channels):
    tap_count, groups = filters.shape
    spread = jnp.broadcast_to(filters[:, :, None], (tap_count, groups, channels // groups))
    return spread.reshape(tap_count, channels).astype(jnp.float32)


def band_matrix(filters, block_rows):
    tap_count, groups = filters.shape
    span_rows = block_rows + tap_count
    repeated = jnp.broadcast_to(jnp.transpose(filters)[:, None, :], (groups, block_rows, tap_count))
    padded = jnp.pad(repeated, ((0, 0), (0, 0), (0, block_rows + 1)))
    flattened = padded.reshape(groups, block_rows * (span_rows + 1))[:, : block_rows * span_rows]
    return flattened.reshape(groups, block_rows, span_rows)


def short_forward(padded_rows, channel_taps, positions, starts):
    tap_count = channel_taps.shape[0]
    row_count = padded_rows.shape[0] - (tap_count - 1)
    accumulated = jnp.zeros((row_count, padded_rows.shape[1]), jnp.float32)
    for offset in range(tap_count):
        shifted = padded_rows[tap_count - 1 - offset : tap_count - 1 - offset + row_count]
        in_doc = (positions - offset >= starts).astype(jnp.float32)[:, None]
        accumulated = accumulated + in_doc * channel_taps[offset][None, :] * shifted.astype(
            jnp.float32
        )
    return accumulated


def short_backward(act_ext, inputs_rows, channel_taps, positions, ext_starts, groups):
    tap_count = channel_taps.shape[0]
    row_count, channels = inputs_rows.shape
    accumulated = jnp.zeros((row_count, channels), jnp.float32)
    tap_terms = []
    for offset in range(tap_count):
        shifted = act_ext[offset : offset + row_count].astype(jnp.float32)
        in_doc = (positions >= ext_starts[offset : offset + row_count]).astype(jnp.float32)[:, None]
        masked = in_doc * shifted
        accumulated = accumulated + channel_taps[offset][None, :] * masked
        product = masked * inputs_rows.astype(jnp.float32)
        tap_terms.append(
            jnp.sum(product.reshape(row_count, groups, channels // groups), axis=(0, 2))
        )
    return (accumulated, jnp.stack(tap_terms))


def long_back(band_table, window, in_document):
    groups, block_rows, span_rows = band_table.shape
    channels = window.shape[1]
    kernel = band_table * in_document.astype(band_table.dtype)[None]
    stacked = window.reshape(span_rows, groups, channels // groups)
    back_grad = jnp.einsum("gst,tgc->sgc", kernel, stacked, preferred_element_type=jnp.float32)
    return back_grad.reshape(block_rows, channels)


def long_terms(band_table, tap_count, cot_ext, gated_rows, first_row, lengths):
    groups, block_rows, span_rows = band_table.shape
    row_count, channels = gated_rows.shape
    group_width = channels // groups
    source_idx = lax.iota(jnp.int32, block_rows)
    target_idx = lax.iota(jnp.int32, span_rows)
    tap_idx = lax.iota(jnp.int32, tap_count)
    diagonal_table = (
        target_idx[None, :, None] - source_idx[:, None, None] == tap_idx[None, None, :]
    ).astype(jnp.float32)

    def one_block(block_index):
        block_start = block_index * block_rows
        window = lax.dynamic_slice_in_dim(cot_ext, block_start, span_rows, 0)
        own_rows = lax.dynamic_slice_in_dim(gated_rows, block_start, block_rows, 0)
        source_pos = first_row + block_start + source_idx
        target_pos = first_row + block_start + target_idx
        in_document = block_mask(lengths, source_pos, target_pos)
        back_grad = long_back(band_table, window, in_document)
        correlation = jnp.einsum(
            "sgc,tgc->gst",
            own_rows.reshape(block_rows, groups, group_width),
            window.reshape(span_rows, groups, group_width),
            preferred_element_type=jnp.float32,
        )
        picker = diagonal_table * in_document.astype(jnp.float32)[:, :, None]
        tap_sums = jnp.einsum("gst,stk->kg", correlation, picker, precision=lax.Precision.HIGHEST)
        return (back_grad, tap_sums)

    back_blocks, tap_blocks = lax.map(
        one_block, jnp.arange(row_count // block_rows, dtype=jnp.int32)
    )
    return (back_blocks.reshape(row_count, channels), jnp.sum(tap_blocks, axis=0))


def on_device(inputs, gates, grad_out, doc_lengths, short_filter, long_filter):
    inputs_rows = inputs[0]
    gate_rows = gates[0]
    cotangent = grad_out[0]
    lengths = doc_lengths[0]
    row_count, channels = inputs_rows.shape
    short_taps, long_taps = (
        lax.all_gather(short_filter, "fsdp", axis=1, tiled=True),
        lax.all_gather(long_filter, "fsdp", axis=1, tiled=True),
    )
    short_count = short_taps.shape[0]
    long_count = long_taps.shape[0]
    groups = long_taps.shape[1]
    short_reach = short_count - 1
    block_rows = 32
    first_row = lax.axis_index("ctx") * row_count
    positions = first_row + lax.iota(jnp.int32, row_count)
    starts = doc_starts(lengths, positions)
    channel_taps = channel_table(short_taps, channels)
    band_table = band_matrix(long_taps, block_rows)
    earlier = passed_along(inputs_rows[row_count - short_reach :], "ctx", 1)
    padded_rows = jnp.concatenate([earlier, inputs_rows], axis=0)
    activation = short_forward(padded_rows, channel_taps, positions, starts).astype(jnp.bfloat16)
    gate_values = gate_rows.astype(jnp.float32)
    gated_rows = (gate_values * activation.astype(jnp.float32)).astype(jnp.bfloat16)
    zero_row = jnp.zeros((1, channels), cotangent.dtype)
    later_rows = passed_along(cotangent[: long_count - 1], "ctx", -1)
    cot_ext = jnp.concatenate([cotangent, later_rows, zero_row], axis=0)
    back_grad, long_part = long_terms(
        band_table, long_count, cot_ext, gated_rows, first_row, lengths
    )
    act_grad = (back_grad * gate_values).astype(jnp.bfloat16)
    act_later = passed_along(act_grad[:short_reach], "ctx", -1)
    grad_gates = (back_grad * activation.astype(jnp.float32)).astype(jnp.bfloat16)
    act_ext = jnp.concatenate([act_grad, act_later], axis=0)
    ext_starts = doc_starts(lengths, first_row + lax.iota(jnp.int32, row_count + short_reach))
    grad_inputs, short_part = short_backward(
        act_ext, inputs_rows, channel_taps, positions, ext_starts, groups
    )
    short_whole, long_whole = lax.psum((short_part, long_part), "ctx")
    short_share, long_share = (
        lax.psum_scatter(short_whole, "fsdp", scatter_dimension=1, tiled=True),
        lax.psum_scatter(long_whole, "fsdp", scatter_dimension=1, tiled=True),
    )
    normalizer = 1.0 / math.sqrt(lax.axis_size("fsdp") * lax.axis_size("ctx") * row_count)
    return (
        grad_inputs.astype(jnp.bfloat16)[None],
        grad_gates[None],
        short_share * normalizer,
        long_share * normalizer,
    )


def solution(mesh):
    placed = (
        P("fsdp", "ctx", None),
        P("fsdp", "ctx", None),
        P("fsdp", "ctx", None),
        P("fsdp", None),
        P(None, "fsdp"),
        P(None, "fsdp"),
    )
    return jax.shard_map(
        on_device,
        mesh=mesh,
        in_specs=placed,
        out_specs=(
            P("fsdp", "ctx", None),
            P("fsdp", "ctx", None),
            P(None, "fsdp"),
            P(None, "fsdp"),
        ),
        check_vma=False,
    )
```

profile of v0, /device:TPU:16, one launch (start us, length us, event | category | flops | bytes accessed | tf_op | source)
XLA Modules:
  0.0 794.8 jit_solution(17697630105618189202)
XLA Ops:
  8.1 3.2 collective-permute-start.1
  11.3 3.3 copy.49
  18.5 10.3 %all-gather = bf16[4,64,7]{1,2,0:T(8,128)(2,1)S(1)} all-gather(bf16[1,64,7]{1,2,0:T(8,128)(2,1)S(1)} %bitcast.129), channel_id=1, replica_groups=mesh['ctx'=64,'fsdp'=4] {'fsdp'}, dimensions={0}, use_global_device_ids=true | all-gather | bytes 4480 | tf_op jit(solution)/shard_map/all_gather | solution.py:121
  32.5 9.6 %all_gather.7 = bf16[128,256]{0,1:T(8,128)(2,1)S(1)} all-gather(bf16[128,64]{0,1:T(8,128)(2,1)} %param.13), channel_id=1, replica_groups=mesh['ctx'=64,'fsdp'=4] {'fsdp'}, dimensions={1}, use_global_device_ids=true | all-gather | bytes 81920 | tf_op jit(solution)/shard_map/all_gather | solution.py:122
  44.2 4.4 reshape.268
  48.6 3.4 slice.175
  52.0 7.8 copy.52
  60.0 8.1 %fusion.26 = (bf16[256,4096]{1,0:T(8,128)(2,1)}, bf16[256,4096]{1,0:T(8,128)(2,1)}) fusion(bf16[1,256,4096]{2,1,0:T(8,128)(2,1)} %param.9, bf16[256,4096]{1,0:T(8,128)(2,1)S(1)} %bitcast.98, bf16[6,4096]{1,0:T(8,128)(2,1)S(1)} %collective-permute-done.1, f32[4096]{0:T(1024)S(1)} %mul.385, f32[256]{0:T(256)S(1)} %copy-done.20, f32[4096]{0:T(1024)S(1)} %mul.380, ...), kind=kLoop, calls=%fused_computation.43 | loop fusion | flops 52428800 | bytes 8559616 | tf_op jit(solution)/shard_map/convert_element_type | solution.py:138
  68.0 3.5 maximum_maximum_fusion
  71.6 232.9 %while.15 = (s32[]{:T(128)}, f32[8,32,4096]{2,1,0:T(8,128)}, f32[8,128,256]{2,1,0:T(8,128)}, s32[8]{0:T(128)S(1)}, bf16[384,4096]{0,1:T(8,128)(2,1)}, /*index=5*...) while((s32[]{:T(128)}, f32[8,32,4096]{2,1,0:T(8,128)}, ...), condition=%wide.region_6.7_spmd.clone, body=%wide.region_4.6_spmd.clone.sunk | while | flops 2099819520 | bytes 22501268 | solution.py:108
  76.2 4.7 fusion.76
  86.7 14.3 %fusion.78 = f32[8,128,256]{2,1,0:T(8,128)} fusion(f32[8,128,256]{2,1,0:T(8,128)} %get-tuple-element.385, s32[]{:T(128)S(6)} %copy.96, f32[256,32,160]{2,1,0:T(8,128)S(1)} %fusion.77, s32[32,160]{1,0:T(8,128)S(1)} %get-tuple-element.409, f32[32,160]{1,0:T(8,128)S(1)} %get-tuple-element.366), kind=kOutput, calls=%fused_computation.14.clone.1 | convolution fusion | flops 2014576640 | bytes 5414916 | tf_op jit(solution)/shard_map/while/body/eval_jaxpr/gst,stk->kg/dot_general | solution.py:105
  105.4 4.7 fusion.76
  115.9 14.3 %fusion.78 = f32[8,128,256]{2,1,0:T(8,128)} fusion(f32[8,128,256]{2,1,0:T(8,128)} %get-tuple-element.385, s32[]{:T(128)S(6)} %copy.96, f32[256,32,160]{2,1,0:T(8,128)S(1)} %fusion.77, s32[32,160]{1,0:T(8,128)S(1)} %get-tuple-element.409, f32[32,160]{1,0:T(8,128)S(1)} %get-tuple-element.366), kind=kOutput, calls=%fused_computation.14.clone.1 | convolution fusion | flops 2014576640 | bytes 5414916 | tf_op jit(solution)/shard_map/while/body/eval_jaxpr/gst,stk->kg/dot_general | solution.py:105
  134.7 4.7 fusion.76
  145.2 14.3 %fusion.78 = f32[8,128,256]{2,1,0:T(8,128)} fusion(f32[8,128,256]{2,1,0:T(8,128)} %get-tuple-element.385, s32[]{:T(128)S(6)} %copy.96, f32[256,32,160]{2,1,0:T(8,128)S(1)} %fusion.77, s32[32,160]{1,0:T(8,128)S(1)} %get-tuple-element.409, f32[32,160]{1,0:T(8,128)S(1)} %get-tuple-element.366), kind=kOutput, calls=%fused_computation.14.clone.1 | convolution fusion | flops 2014576640 | bytes 5414916 | tf_op jit(solution)/shard_map/while/body/eval_jaxpr/gst,stk->kg/dot_general | solution.py:105
  163.9 4.7 fusion.76
  174.4 14.3 %fusion.78 = f32[8,128,256]{2,1,0:T(8,128)} fusion(f32[8,128,256]{2,1,0:T(8,128)} %get-tuple-element.385, s32[]{:T(128)S(6)} %copy.96, f32[256,32,160]{2,1,0:T(8,128)S(1)} %fusion.77, s32[32,160]{1,0:T(8,128)S(1)} %get-tuple-element.409, f32[32,160]{1,0:T(8,128)S(1)} %get-tuple-element.366), kind=kOutput, calls=%fused_computation.14.clone.1 | convolution fusion | flops 2014576640 | bytes 5414916 | tf_op jit(solution)/shard_map/while/body/eval_jaxpr/gst,stk->kg/dot_general | solution.py:105
  192.8 4.7 fusion.76
  203.4 14.3 %fusion.78 = f32[8,128,256]{2,1,0:T(8,128)} fusion(f32[8,128,256]{2,1,0:T(8,128)} %get-tuple-element.385, s32[]{:T(128)S(6)} %copy.96, f32[256,32,160]{2,1,0:T(8,128)S(1)} %fusion.77, s32[32,160]{1,0:T(8,128)S(1)} %get-tuple-element.409, f32[32,160]{1,0:T(8,128)S(1)} %get-tuple-element.366), kind=kOutput, calls=%fused_computation.14.clone.1 | convolution fusion | flops 2014576640 | bytes 5414916 | tf_op jit(solution)/shard_map/while/body/eval_jaxpr/gst,stk->kg/dot_general | solution.py:105
  221.8 4.7 fusion.76
  232.3 14.3 %fusion.78 = f32[8,128,256]{2,1,0:T(8,128)} fusion(f32[8,128,256]{2,1,0:T(8,128)} %get-tuple-element.385, s32[]{:T(128)S(6)} %copy.96, f32[256,32,160]{2,1,0:T(8,128)S(1)} %fusion.77, s32[32,160]{1,0:T(8,128)S(1)} %get-tuple-element.409, f32[32,160]{1,0:T(8,128)S(1)} %get-tuple-element.366), kind=kOutput, calls=%fused_computation.14.clone.1 | convolution fusion | flops 2014576640 | bytes 5414916 | tf_op jit(solution)/shard_map/while/body/eval_jaxpr/gst,stk->kg/dot_general | solution.py:105
  250.7 4.7 fusion.76
  261.2 14.3 %fusion.78 = f32[8,128,256]{2,1,0:T(8,128)} fusion(f32[8,128,256]{2,1,0:T(8,128)} %get-tuple-element.385, s32[]{:T(128)S(6)} %copy.96, f32[256,32,160]{2,1,0:T(8,128)S(1)} %fusion.77, s32[32,160]{1,0:T(8,128)S(1)} %get-tuple-element.409, f32[32,160]{1,0:T(8,128)S(1)} %get-tuple-element.366), kind=kOutput, calls=%fused_computation.14.clone.1 | convolution fusion | flops 2014576640 | bytes 5414916 | tf_op jit(solution)/shard_map/while/body/eval_jaxpr/gst,stk->kg/dot_general | solution.py:105
  279.7 4.7 fusion.76
  290.2 14.3 %fusion.78 = f32[8,128,256]{2,1,0:T(8,128)} fusion(f32[8,128,256]{2,1,0:T(8,128)} %get-tuple-element.385, s32[]{:T(128)S(6)} %copy.96, f32[256,32,160]{2,1,0:T(8,128)S(1)} %fusion.77, s32[32,160]{1,0:T(8,128)S(1)} %get-tuple-element.409, f32[32,160]{1,0:T(8,128)S(1)} %get-tuple-element.366), kind=kOutput, calls=%fused_computation.14.clone.1 | convolution fusion | flops 2014576640 | bytes 5414916 | tf_op jit(solution)/shard_map/while/body/eval_jaxpr/gst,stk->kg/dot_general | solution.py:105
  304.6 6.2 fusion.27
  318.3 14.9 %fusion.40 = (f32[4096]{0:T(1024)S(1)}, f32[4096]{0:T(1024)S(1)}, f32[4096]{0:T(1024)S(1)}, f32[4096]{0:T(1024)S(1)}, f32[4096]{0:T(1024)S(1)}, /*index=5*/f32[4096]{0:T(1024)S(1)}) fusion(bf16[6,4096]{1,0:T(8,128)(2,1)S(1)} %collective-permute-done.2, bf16[256,4096]{1,0:T(8,128)(2,1)} %copy-done.2, f32[256]{0:T(256)} %get-tuple-element.283, ...), kind=kLoop, calls=%fused_computation.57 | loop fusion | flops 45064192 | bytes 4347904 | tf_op jit(solution)/shard_map/reduce_sum | solution.py:65
  337.0 9.7 %fusion.53 = bf16[1,256,4096]{2,1,0:T(8,128)(2,1)} fusion(bf16[6,4096]{1,0:T(8,128)(2,1)S(1)} %collective-permute-done.2, bf16[256,4096]{1,0:T(8,128)(2,1)S(1)} %copy-done.3, f32[256]{0:T(256)} %get-tuple-element.283, f32[4096]{0:T(1024)S(1)} %mul.385, f32[256]{0:T(256)} %get-tuple-element.284, f32[4096]{0:T(1024)S(1)} %mul.380, f32[256]{0:T(256)} %get-tuple-element.285, ...), kind=kLoop, calls=%fused_computation.86 | loop fusion | flops 48234496 | bytes 4365312 | tf_op jit(solution)/shard_map/broadcast_in_dim | solution.py:160
  346.6 46.6 %reduce-scatter.7.cloned.1.call-done = f32[64,7]{1,0:T(8,128)} async-done(((f32[256,7]{1,0:T(8,128)}), f32[64,7]{1,0:T(8,128)}) %reduce-scatter.7.cloned.1.call-update) | async-done | bytes 1808
  394.0 33.4 %reduce-scatter.9.cloned.1.call-done = f32[64,128]{1,0:T(8,128)} async-done(((f32[256,128]{1,0:T(8,128)}), f32[64,128]{1,0:T(8,128)}) %reduce-scatter.9.cloned.1.call-update) | async-done | bytes 32784
  428.3 358.4 %all-reduce.1 = (f32[7,64]{1,0:T(8,128)S(1)}, f32[128,64]{1,0:T(8,128)S(1)}) all-reduce(f32[7,64]{1,0:T(8,128)S(1)} %copy.58, f32[128,64]{1,0:T(8,128)S(1)} %copy.60), channel_id=1, replica_groups=mesh['ctx'=64,'fsdp'=4] {'ctx'}, use_global_device_ids=true, to_apply=%region_21.22 | all-reduce | flops 8640 | bytes 69120 | tf_op jit(solution)/shard_map/psum | solution.py:153
  (276 shorter events, 99.5 us)
Async XLA Ops:
  7.2 386.0 %reduce-scatter.7.cloned.1.call-start = ((), (), s32[]{:S(2)}) async-start(), calls=%async_computation.2 | async-start | bytes 163840
  8.1 51.8 %collective-permute-start.1 = (bf16[6,4096]{1,0:T(8,128)(2,1)S(1)}, bf16[6,4096]{1,0:T(8,128)(2,1)S(1)}, u32[]{:S(2)}, u32[]{:S(2)}) collective-permute-start(bf16[6,4096]{1,0:T(8,128)(2,1)S(1)} %slice_bitcast_fusion.1), channel_id=1, source_target_pairs={{0,4},{4,8},{8,12},{12,16},{16,20},{20,24},{24,28},{28,32},{32,36}... | collective-permute-start | bytes 147464 | tf_op jit(solution)/shard_map/ppermute | solution.py:12
  14.6 29.6 %copy-start.6 = (bf16[1,256,4096]{1,2,0:T(8,128)(2,1)}, bf16[1,256,4096]{1,2,0:T(8,128)(2,1)S(1)}, u32[]{:S(2)}) copy-start(bf16[1,256,4096]{1,2,0:T(8,128)(2,1)S(1)} %copy.49) | copy-start | bytes 6291460
  14.7 53.4 %collective-permute-start = (bf16[127,4096]{0,1:T(8,128)(2,1)S(1)}, bf16[127,4096]{0,1:T(8,128)(2,1)}, u32[]{:S(2)}, u32[]{:S(2)}) collective-permute-start(bf16[127,4096]{0,1:T(8,128)(2,1)S(1)} %slice_bitcast_fusion), channel_id=1, source_target_pairs={{4,0},{8,4},{12,8},{16,12},{20,16},{24,20},{28,24},{32,28},{36,32}... | collective-permute-start | bytes 3121160 | tf_op jit(solution)/shard_map/ppermute | solution.py:12
  32.3 27.6 %copy-start.9 = (f32[4096]{0:T(1024)}, f32[4096]{0:T(1024)S(1)}, u32[]{:S(2)}) copy-start(f32[4096]{0:T(1024)S(1)} %mul.360) | copy-start | bytes 49156
  32.5 27.4 %copy-start.11 = (f32[4096]{0:T(1024)}, f32[4096]{0:T(1024)S(1)}, u32[]{:S(2)}) copy-start(f32[4096]{0:T(1024)S(1)} %mul.347) | copy-start | bytes 49156
  86.7 14.4 %copy-start.15 = (s32[1,64]{1,0:T(1,128)S(1)}, s32[1,64]{1,0:T(1,128)}, u32[]{:S(2)}) copy-start(s32[1,64]{1,0:T(1,128)} %get-tuple-element.442) | copy-start | bytes 772 | tf_op jit(solution)/shard_map/while
  86.7 14.3 %copy-start.18 = (s32[1,64]{1,0:T(1,128)S(1)}, s32[1,64]{1,0:T(1,128)}, u32[]{:S(2)}) copy-start(s32[1,64]{1,0:T(1,128)} %get-tuple-element.462) | copy-start | bytes 772 | tf_op jit(solution)/shard_map/while
  86.7 14.3 %copy-start.28 = (s32[8]{0:T(128)S(1)}, s32[8]{0:T(128)}, u32[]{:S(2)}) copy-start(s32[8]{0:T(128)} %copy-done.27) | copy-start | bytes 100 | tf_op jit(solution)/shard_map/while
  115.9 14.4 %copy-start.15 = (s32[1,64]{1,0:T(1,128)S(1)}, s32[1,64]{1,0:T(1,128)}, u32[]{:S(2)}) copy-start(s32[1,64]{1,0:T(1,128)} %get-tuple-element.442) | copy-start | bytes 772 | tf_op jit(solution)/shard_map/while
  115.9 14.3 %copy-start.18 = (s32[1,64]{1,0:T(1,128)S(1)}, s32[1,64]{1,0:T(1,128)}, u32[]{:S(2)}) copy-start(s32[1,64]{1,0:T(1,128)} %get-tuple-element.462) | copy-start | bytes 772 | tf_op jit(solution)/shard_map/while
  115.9 14.3 %copy-start.28 = (s32[8]{0:T(128)S(1)}, s32[8]{0:T(128)}, u32[]{:S(2)}) copy-start(s32[8]{0:T(128)} %copy-done.27) | copy-start | bytes 100 | tf_op jit(solution)/shard_map/while
  145.2 14.3 %copy-start.15 = (s32[1,64]{1,0:T(1,128)S(1)}, s32[1,64]{1,0:T(1,128)}, u32[]{:S(2)}) copy-start(s32[1,64]{1,0:T(1,128)} %get-tuple-element.442) | copy-start | bytes 772 | tf_op jit(solution)/shard_map/while
  145.2 14.3 %copy-start.18 = (s32[1,64]{1,0:T(1,128)S(1)}, s32[1,64]{1,0:T(1,128)}, u32[]{:S(2)}) copy-start(s32[1,64]{1,0:T(1,128)} %get-tuple-element.462) | copy-start | bytes 772 | tf_op jit(solution)/shard_map/while
  174.4 14.3 %copy-start.15 = (s32[1,64]{1,0:T(1,128)S(1)}, s32[1,64]{1,0:T(1,128)}, u32[]{:S(2)}) copy-start(s32[1,64]{1,0:T(1,128)} %get-tuple-element.442) | copy-start | bytes 772 | tf_op jit(solution)/shard_map/while
  174.4 14.3 %copy-start.18 = (s32[1,64]{1,0:T(1,128)S(1)}, s32[1,64]{1,0:T(1,128)}, u32[]{:S(2)}) copy-start(s32[1,64]{1,0:T(1,128)} %get-tuple-element.462) | copy-start | bytes 772 | tf_op jit(solution)/shard_map/while
  203.3 14.4 %copy-start.15 = (s32[1,64]{1,0:T(1,128)S(1)}, s32[1,64]{1,0:T(1,128)}, u32[]{:S(2)}) copy-start(s32[1,64]{1,0:T(1,128)} %get-tuple-element.442) | copy-start | bytes 772 | tf_op jit(solution)/shard_map/while
  203.3 14.3 %copy-start.18 = (s32[1,64]{1,0:T(1,128)S(1)}, s32[1,64]{1,0:T(1,128)}, u32[]{:S(2)}) copy-start(s32[1,64]{1,0:T(1,128)} %get-tuple-element.462) | copy-start | bytes 772 | tf_op jit(solution)/shard_map/while
  203.3 14.3 %copy-start.28 = (s32[8]{0:T(128)S(1)}, s32[8]{0:T(128)}, u32[]{:S(2)}) copy-start(s32[8]{0:T(128)} %copy-done.27) | copy-start | bytes 100 | tf_op jit(solution)/shard_map/while
  232.2 14.4 %copy-start.15 = (s32[1,64]{1,0:T(1,128)S(1)}, s32[1,64]{1,0:T(1,128)}, u32[]{:S(2)}) copy-start(s32[1,64]{1,0:T(1,128)} %get-tuple-element.442) | copy-start | bytes 772 | tf_op jit(solution)/shard_map/while
  232.3 14.4 %copy-start.18 = (s32[1,64]{1,0:T(1,128)S(1)}, s32[1,64]{1,0:T(1,128)}, u32[]{:S(2)}) copy-start(s32[1,64]{1,0:T(1,128)} %get-tuple-element.462) | copy-start | bytes 772 | tf_op jit(solution)/shard_map/while
  232.3 14.3 %copy-start.28 = (s32[8]{0:T(128)S(1)}, s32[8]{0:T(128)}, u32[]{:S(2)}) copy-start(s32[8]{0:T(128)} %copy-done.27) | copy-start | bytes 100 | tf_op jit(solution)/shard_map/while
  261.2 14.4 %copy-start.15 = (s32[1,64]{1,0:T(1,128)S(1)}, s32[1,64]{1,0:T(1,128)}, u32[]{:S(2)}) copy-start(s32[1,64]{1,0:T(1,128)} %get-tuple-element.442) | copy-start | bytes 772 | tf_op jit(solution)/shard_map/while
  261.2 14.3 %copy-start.18 = (s32[1,64]{1,0:T(1,128)S(1)}, s32[1,64]{1,0:T(1,128)}, u32[]{:S(2)}) copy-start(s32[1,64]{1,0:T(1,128)} %get-tuple-element.462) | copy-start | bytes 772 | tf_op jit(solution)/shard_map/while
  261.2 14.3 %copy-start.28 = (s32[8]{0:T(128)S(1)}, s32[8]{0:T(128)}, u32[]{:S(2)}) copy-start(s32[8]{0:T(128)} %copy-done.27) | copy-start | bytes 100 | tf_op jit(solution)/shard_map/while
  290.1 14.4 %copy-start.15 = (s32[1,64]{1,0:T(1,128)S(1)}, s32[1,64]{1,0:T(1,128)}, u32[]{:S(2)}) copy-start(s32[1,64]{1,0:T(1,128)} %get-tuple-element.442) | copy-start | bytes 772 | tf_op jit(solution)/shard_map/while
  290.2 14.3 %copy-start.18 = (s32[1,64]{1,0:T(1,128)S(1)}, s32[1,64]{1,0:T(1,128)}, u32[]{:S(2)}) copy-start(s32[1,64]{1,0:T(1,128)} %get-tuple-element.462) | copy-start | bytes 772 | tf_op jit(solution)/shard_map/while
  312.1 6.2 collective-permute-start.2
  315.5 20.6 %copy-start.8 = (f32[8,128,256]{2,1,0:T(8,128)S(1)}, f32[8,128,256]{2,1,0:T(8,128)}, u32[]{:S(2)}) copy-start(f32[8,128,256]{2,1,0:T(8,128)} %get-tuple-element.447) | copy-start | bytes 3145732
  315.5 21.4 %copy-start.10 = (f32[4096]{0:T(1024)S(1)}, f32[4096]{0:T(1024)}, u32[]{:S(2)}) copy-start(f32[4096]{0:T(1024)} %copy-done.9) | copy-start | bytes 49156
  315.5 21.4 %copy-start.12 = (f32[4096]{0:T(1024)S(1)}, f32[4096]{0:T(1024)}, u32[]{:S(2)}) copy-start(f32[4096]{0:T(1024)} %copy-done.11) | copy-start | bytes 49156
  336.0 91.4 %reduce-scatter.9.cloned.1.call-start = ((), (), s32[]{:S(2)}) async-start(), calls=%async_computation.3 | async-start | bytes 163840
  (30 other events, 259.5 us)
Sparse Core Ops, SparseCore 0:
  336.2 56.9 reduce-scatter.6
  396.1 31.3 reduce-scatter.8
where the time goes:
time: 802 us; the launch traced here: 795 us
  blocking collectives  378 us (47%)
  matrix products  163 us (20%)
  local copies, waits for them, and re-layouts  93.2 us (12%)
  waiting for transfers between devices  82 us (10%)
  other arithmetic  49.8 us (6%)
  between operations  14.7 us (2%)
  starting transfers between devices  8.27 us (1%)
    psum x1, blocking collectives, on_device(): short_whole, long_whole = lax.psum((short_part, long_part), 'ctx')  358 us
    dot_general x8, matrix products, one_block(): jnp.einsum('gst,stk->kg', correlation, picker, precision=lax.Precision.HI...  115 us
    unnamed x4, waiting for transfers between devices  80 us
    dot_general x8, matrix products, long_back(): jnp.einsum('gst,tgc->sgc', kernel, stacked, preferred_element_type=jnp.fl...  37.7 us
    dynamic_update_slice x16, local copies, waits for them, and re-layouts, long_terms(): lax.map(one_block, jnp.arange(row_count // block_rows, dtype=jnp.int32))  24.1 us
    dynamic_slice x8, local copies, waits for them, and re-layouts, one_block(): window = lax.dynamic_slice_in_dim(cot_ext, block_start, span_rows, 0)  22.5 us
    reduce_sum x9, other arithmetic, short_backward(): jnp.sum(product.reshape(row_count, groups, channels // groups), axis=(0, 2))  17.2 us
    unnamed x57, local copies, waits for them, and re-layouts  16.4 us
  transfers between devices with their start and end apart: 5, of which 3 were waited for; matrix products, arithmetic and copies ran while one was open for 6% of the time, Pallas kernels for 0%

commit v1 on v0

v1 whole, which is shorter than its diff:
```python
import functools
import math

import jax
import jax.numpy as jnp
from jax import lax
from jax.experimental import pallas as pl
from jax.experimental.pallas import tpu as pltpu
from jax.sharding import PartitionSpec as P

MESH = pl.DeviceIdType.MESH
F32 = jnp.float32
BF16 = jnp.bfloat16

LANES = 128
TAPS = 128
SHORT = 7
BLOCK = 128
HALO = 144
EXT = 16
WIDTH = 16
PER = LANES // WIDTH
FILT = 80
PART = 72


def ring(axis, distance):
    n = lax.axis_size(axis)
    return lax.rem(lax.axis_index(axis) + distance + n, n)


def entry_kernel(
    inputs, gates, cot, short_ref, long_ref, filt_out, in_out, gate_out, cot_out,
    mine, own_sem, send_sem, recv_sem,
):
    rows = inputs.shape[1]
    peers = lax.axis_size("fsdp")
    f = lax.axis_index("fsdp")
    after, before = ring("ctx", 1), ring("ctx", -1)
    barrier = pltpu.get_barrier_semaphore()
    for to in (after, before):
        pl.semaphore_signal(barrier, inc=1, device_id=(to, f), device_id_type=MESH)
    for d in range(1, peers):
        pl.semaphore_signal(
            barrier, inc=1, device_id=(lax.axis_index("ctx"), ring("fsdp", d)), device_id_type=MESH
        )
    mine[...] = jnp.zeros_like(mine)
    mine[0:64, :] = jnp.transpose(long_ref[...].astype(F32)).astype(BF16)
    mine[64 : 64 + SHORT, 0:64] = short_ref[...]
    pl.semaphore_wait(barrier, peers + 1)
    copies = []
    for d in range(1, peers):
        copies.append(
            pltpu.make_async_remote_copy(
                mine, filt_out.at[f], send_sem.at[d], recv_sem.at[d],
                device_id=(lax.axis_index("ctx"), ring("fsdp", d)), device_id_type=MESH,
            )
        )
    copies.append(
        pltpu.make_async_remote_copy(
            inputs.at[0, pl.ds(rows - 16, 16), :], in_out, send_sem.at[4], recv_sem.at[4],
            device_id=(after, f), device_id_type=MESH,
        )
    )
    copies.append(
        pltpu.make_async_remote_copy(
            gates.at[0, pl.ds(0, EXT), :], gate_out, send_sem.at[5], recv_sem.at[5],
            device_id=(before, f), device_id_type=MESH,
        )
    )
    copies.append(
        pltpu.make_async_remote_copy(
            cot.at[0, pl.ds(0, HALO), :], cot_out, send_sem.at[6], recv_sem.at[6],
            device_id=(before, f), device_id_type=MESH,
        )
    )
    for c in copies:
        c.start()
    own = pltpu.make_async_copy(mine, filt_out.at[f], own_sem)
    own.start()
    own.wait()
    for c in copies:
        c.wait()


def entry(inputs, gates, cot, short_filter, long_filter):
    channels = inputs.shape[2]
    peers = lax.axis_size("fsdp")
    anyspace = pl.BlockSpec(memory_space=pl.ANY)
    vmem = pl.BlockSpec(memory_space=pltpu.VMEM)
    return pl.pallas_call(
        entry_kernel,
        out_shape=(
            jax.ShapeDtypeStruct((peers, FILT, LANES), BF16),
            jax.ShapeDtypeStruct((16, channels), BF16),
            jax.ShapeDtypeStruct((EXT, channels), BF16),
            jax.ShapeDtypeStruct((HALO, channels), BF16),
        ),
        in_specs=[anyspace, anyspace, anyspace, vmem, vmem],
        out_specs=(anyspace, anyspace, anyspace, anyspace),
        scratch_shapes=[
            pltpu.VMEM((FILT, LANES), BF16),
            pltpu.SemaphoreType.DMA,
            pltpu.SemaphoreType.DMA((7,)),
            pltpu.SemaphoreType.DMA((7,)),
        ],
        compiler_params=pltpu.CompilerParams(collective_id=0, has_side_effects=True),
        name="entry",
    )(inputs, gates, cot, short_filter, long_filter)


def prepare(lengths, filt, filt32, win_mask, ext_mask, diag_mask, fwd_mask, bwd_mask, rcol, cot_s, row0):
    docs = lengths.shape[1]
    rows = fwd_mask.shape[1]
    lane_pos = row0 + lax.broadcasted_iota(jnp.int32, (8, 512), 1)
    row_pos = row0 + lax.broadcasted_iota(jnp.int32, rcol.shape, 0)

    def one_doc(d, carry):
        end, lane_start, row_start = carry
        end = end + lengths[0, d]
        return (
            end,
            jnp.where(lane_pos >= end, end, lane_start),
            jnp.where(row_pos >= end, end, row_start),
        )

    _, lane_start, row_start = lax.fori_loop(
        0, docs, one_doc,
        (jnp.int32(0), jnp.zeros((8, 512), jnp.int32), jnp.zeros(rcol.shape, jnp.int32)),
    )
    rcol[...] = (row_pos - row_start).astype(F32)
    for j in range(1, SHORT):
        fwd_mask[j - 1] = (rcol[0:rows, :] >= j).astype(F32)
        bwd_mask[j - 1] = (rcol[j : j + rows, :] >= j).astype(F32)
    s_rel = lax.broadcasted_iota(jnp.int32, (BLOCK, LANES), 0)
    lane = lax.broadcasted_iota(jnp.int32, (BLOCK, LANES), 1)
    near = lane >= s_rel
    for b in range(rows // BLOCK):
        s_abs = row0 + b * BLOCK + s_rel
        t0 = jnp.broadcast_to(lane_start[0:1, b * BLOCK : b * BLOCK + LANES], (BLOCK, LANES))
        t1 = jnp.broadcast_to(
            lane_start[0:1, (b + 1) * BLOCK : (b + 1) * BLOCK + LANES], (BLOCK, LANES)
        )
        m0 = jnp.where(near & (t0 <= s_abs), 1.0, 0.0).astype(F32)
        m1 = jnp.where(jnp.logical_not(near) & (t1 <= s_abs), 1.0, 0.0).astype(F32)
        win_mask[b, :, 0:LANES] = m0.astype(BF16)
        win_mask[b, :, LANES:] = m1.astype(BF16)
        diag_mask[b] = m0 + m1
    s_abs = row0 + rows + s_rel[0:EXT]
    t0 = jnp.broadcast_to(lane_start[0:1, rows : rows + LANES], (EXT, LANES))
    t1 = jnp.broadcast_to(lane_start[0:1, rows + LANES : rows + 2 * LANES], (EXT, LANES))
    m0 = jnp.where(near[0:EXT] & (t0 <= s_abs), 1.0, 0.0).astype(F32)
    m1 = jnp.where(jnp.logical_not(near[0:EXT]) & (t1 <= s_abs), 1.0, 0.0).astype(F32)
    ext_mask[:, 0:LANES] = m0.astype(BF16)
    ext_mask[:, LANES:] = m1.astype(BF16)
    filt32[...] = filt[...].astype(F32)
    cot_s[rows + HALO :, :] = jnp.zeros((cot_s.shape[0] - rows - HALO, LANES), BF16)


def compute_kernel(
    lengths, filt, inputs, in_before, gates, gates_after, cot, cot_after,
    gin_out, ggate_out, part_out,
    filt32, win_mask, ext_mask, diag_mask, fwd_mask, bwd_mask, rcol,
    cot_s, x_s, act_s, gate_s, ag_s, gated_m, table, ext_table, corr, back_all, back_ext,
):
    rows = inputs.shape[1]
    blocks = rows // BLOCK
    q = pl.program_id(0)
    row0 = lax.axis_index("ctx") * rows

    @pl.when(q == 0)
    def _():
        prepare(
            lengths, filt, filt32, win_mask, ext_mask, diag_mask, fwd_mask, bwd_mask, rcol, cot_s, row0
        )
        part_out[...] = jnp.zeros_like(part_out)

    per_share = 64 // PER
    share, at = q // per_share, lax.rem(q, per_share)
    lane_group = lax.broadcasted_iota(jnp.int32, (BLOCK, LANES), 1) // WIDTH
    spread = (
        lax.broadcasted_iota(jnp.int32, (LANES, LANES), 0)
        == at * PER + lax.broadcasted_iota(jnp.int32, (LANES, LANES), 1) // WIDTH
    ).astype(F32)
    taps = jnp.dot(
        filt32[share, 64:72, :].astype(BF16), spread.astype(BF16), preferred_element_type=F32
    )
    long_rows = filt32[share, pl.ds(pl.multiple_of(at * PER, PER), PER), :]

    cot_s[0:rows, :] = cot[0]
    cot_s[rows : rows + HALO, :] = cot_after[...]
    x_s[0:8, :] = in_before[...].astype(F32)[8:16]
    x_s[8:, :] = inputs[0].astype(F32)
    gate_s[0:rows, :] = gates[0].astype(F32)
    gate_s[rows:, :] = gates_after[...].astype(F32)

    act = taps[0:1, :] * x_s[8 : 8 + rows, :]
    for j in range(1, SHORT):
        act = act + fwd_mask[j - 1] * (taps[j : j + 1, :] * x_s[8 - j : 8 - j + rows, :])
    act = act.astype(BF16).astype(F32)
    act_s[...] = act
    gated = (gate_s[0:rows, :] * act).astype(BF16)

    for g in range(PER):
        circ = pltpu.roll(
            jnp.broadcast_to(long_rows[g : g + 1, :], (BLOCK, LANES)), 0, 1, stride=1, stride_axis=0
        ).astype(BF16)
        both = jnp.concatenate([circ, circ], axis=1)
        for b in range(blocks):
            table[b, g * BLOCK : (g + 1) * BLOCK, :] = both * win_mask[b]
        ext_table[g * EXT : (g + 1) * EXT, :] = both[0:EXT] * ext_mask[...]
        for b in range(blocks):
            gated_m[b, g * BLOCK : (g + 1) * BLOCK, :] = jnp.where(
                lane_group == g, gated[b * BLOCK : (b + 1) * BLOCK, :], jnp.zeros((), BF16)
            )
    for b in range(blocks):
        window = cot_s[b * BLOCK : (b + 2) * BLOCK, :]
        back_all[...] = jnp.dot(table[b], window, preferred_element_type=F32)
        back = back_all[0:BLOCK, :]
        for g in range(1, PER):
            back = jnp.where(lane_group == g, back_all[g * BLOCK : (g + 1) * BLOCK, :], back)
        own = slice(b * BLOCK, (b + 1) * BLOCK)
        ag_s[own, :] = (back * gate_s[own, :]).astype(BF16).astype(F32)
        ggate_out[0, own, :] = (back * act_s[own, :]).astype(BF16)
        corr[b] = lax.dot_general(
            gated_m[b], window, (((1,), (1,)), ((), ())), preferred_element_type=F32
        )
    back_ext[...] = jnp.dot(
        ext_table[...], cot_s[rows : rows + 2 * BLOCK, :], preferred_element_type=F32
    )
    back = back_ext[0:EXT, :]
    for g in range(1, PER):
        back = jnp.where(lane_group[0:EXT] == g, back_ext[g * EXT : (g + 1) * EXT, :], back)
    ag_s[rows:, :] = (back * gate_s[rows:, :]).astype(BF16).astype(F32)

    gin = jnp.zeros((rows, LANES), F32)
    terms = []
    for j in range(SHORT):
        moved = ag_s[j : j + rows, :]
        if j:
            moved = bwd_mask[j - 1] * moved
        gin = gin + taps[j : j + 1, :] * moved
        terms.append(jnp.sum(moved * x_s[8 : 8 + rows, :], axis=0, keepdims=True))
    gin_out[0] = gin.astype(BF16)
    terms.append(jnp.zeros((1, LANES), F32))
    gathered = (
        lax.broadcasted_iota(jnp.int32, (LANES, LANES), 1)
        == at * PER + lax.broadcasted_iota(jnp.int32, (LANES, LANES), 0) // WIDTH
    ).astype(F32)
    part_out[share, 64:72, :] += jnp.dot(
        jnp.concatenate(terms, axis=0), gathered,
        preferred_element_type=F32, precision=lax.Precision.HIGHEST,
    )

    lane8 = lax.broadcasted_iota(jnp.int32, (8, LANES), 1)
    row8 = lax.broadcasted_iota(jnp.int32, (8, LANES), 0)
    tap_rows = []
    for g in range(PER):
        total = jnp.zeros((8, LANES), F32)
        for i in range(BLOCK // 8):
            near = lane8 >= row8 + 8 * i
            at_row = g * BLOCK + 8 * i
            merged = jnp.zeros((8, LANES), F32)
            for b in range(blocks):
                merged = merged + diag_mask[b, 8 * i : 8 * i + 8, :] * jnp.where(
                    near,
                    corr[b, at_row : at_row + 8, 0:LANES],
                    corr[b, at_row : at_row + 8, LANES:],
                )
            total = total + (pltpu.roll(merged, LANES - 8 * i, 1) if i else merged)
        for bit in (1, 2, 4):
            total = jnp.where((row8 & bit) > 0, pltpu.roll(total, LANES - bit, 1), total)
        tap_rows.append(jnp.sum(total, axis=0, keepdims=True))
    part_out[share, pl.ds(pl.multiple_of(at * PER, PER), PER), :] = jnp.concatenate(
        tap_rows, axis=0
    )


def compute(lengths, filt, inputs, in_before, gates, gates_after, cot, cot_after):
    _, rows, channels = inputs.shape
    shares = filt.shape[0]
    blocks = rows // BLOCK
    whole = pl.BlockSpec((1, rows, LANES), lambda q: (0, 0, q))
    return pl.pallas_call(
        compute_kernel,
        grid=(channels // LANES,),
        out_shape=(
            jax.ShapeDtypeStruct(inputs.shape, BF16),
            jax.ShapeDtypeStruct(inputs.shape, BF16),
            jax.ShapeDtypeStruct((shares, PART, LANES), F32),
        ),
        in_specs=[
            pl.BlockSpec(memory_space=pltpu.SMEM),
            pl.BlockSpec((shares, FILT, LANES), lambda q: (0, 0, 0)),
            whole,
            pl.BlockSpec((16, LANES), lambda q: (0, q)),
            whole,
            pl.BlockSpec((EXT, LANES), lambda q: (0, q)),
            whole,
            pl.BlockSpec((HALO, LANES), lambda q: (0, q)),
        ],
        out_specs=(whole, whole, pl.BlockSpec((shares, PART, LANES), lambda q: (0, 0, 0))),
        scratch_shapes=[
            pltpu.VMEM((shares, FILT, LANES), F32),
            pltpu.VMEM((blocks, BLOCK, 2 * LANES), BF16),
            pltpu.VMEM((EXT, 2 * LANES), BF16),
            pltpu.VMEM((blocks, BLOCK, LANES), F32),
            pltpu.VMEM((SHORT - 1, rows, LANES), F32),
            pltpu.VMEM((SHORT - 1, rows, LANES), F32),
            pltpu.VMEM((rows + EXT, LANES), F32),
            pltpu.VMEM((rows + 2 * BLOCK, LANES), BF16),
            pltpu.VMEM((rows + 8, LANES), F32),
            pltpu.VMEM((rows, LANES), F32),
            pltpu.VMEM((rows + EXT, LANES), F32),
            pltpu.VMEM((rows + EXT, LANES), F32),
            pltpu.VMEM((blocks, PER * BLOCK, LANES), BF16),
            pltpu.VMEM((blocks, PER * BLOCK, 2 * LANES), BF16),
            pltpu.VMEM((PER * EXT, 2 * LANES), BF16),
            pltpu.VMEM((blocks, PER * BLOCK, 2 * LANES), F32),
            pltpu.VMEM((PER * BLOCK, LANES), F32),
            pltpu.VMEM((PER * EXT, LANES), F32),
        ],
        compiler_params=pltpu.CompilerParams(vmem_limit_bytes=40 << 20),
        name="layer_pair",
    )(lengths, filt, inputs, in_before, gates, gates_after, cot, cot_after)


def reduce_kernel(scale, part, short_out, long_out, bufs, cur, send_sem, recv_sem):
    side = 4
    f = lax.axis_index("fsdp")
    ctx = lax.axis_index("ctx")
    y, zl, x = lax.rem(ctx, side), lax.rem(ctx // side, side), ctx // (side * side)

    def peer(phase, d):
        if phase == 0:
            return (ctx, lax.rem(f + d, side))
        stride = (1, side * side, side)[phase - 1]
        at = (y, x, zl)[phase - 1]
        return (ctx + (lax.rem(at + d, side) - at) * stride, f)

    places = (f, y, x, zl)
    barrier = pltpu.get_barrier_semaphore()
    for phase in range(4):
        for d in range(1, side):
            pl.semaphore_signal(barrier, inc=1, device_id=peer(phase, d), device_id_type=MESH)
    pl.semaphore_wait(barrier, 4 * (side - 1))
    for phase in range(4):
        me = places[phase]
        copies = []
        for d in range(1, side):
            source = part.at[lax.rem(f + d, side)] if phase == 0 else cur.at[phase]
            copies.append(
                pltpu.make_async_remote_copy(
                    source, bufs.at[phase, side - d], send_sem.at[phase, d],
                    recv_sem.at[phase, side - d],
                    device_id=peer(phase, d), device_id_type=MESH,
                )
            )
        for c in copies:
            c.start()
        mine = part[f] if phase == 0 else cur[phase]
        for d in range(1, side):
            pltpu.make_async_remote_copy(
                cur.at[phase], bufs.at[phase, d], send_sem.at[phase, d], recv_sem.at[phase, d],
                device_id=peer(phase, d), device_id_type=MESH,
            ).wait_recv()
        bufs[phase, 0] = mine
        total = jnp.zeros(mine.shape, F32)
        for place in range(side):
            total = total + bufs[phase, lax.rem(place - me + side, side)]
        for c in copies:
            c.wait_send()
        if phase < 3:
            cur[phase + 1] = total
    total = total * scale
    wide = jnp.concatenate([total[0:64], jnp.zeros((64, LANES), F32)], axis=0)
    long_out[...] = jnp.transpose(wide)[:, 0:64]
    short_out[...] = total[64 : 64 + SHORT, 0:64]


def reduce(part, scale, short_shape, long_shape):
    vmem = pl.BlockSpec(memory_space=pltpu.VMEM)
    return pl.pallas_call(
        functools.partial(reduce_kernel, scale),
        out_shape=(
            jax.ShapeDtypeStruct(short_shape, F32),
            jax.ShapeDtypeStruct(long_shape, F32),
        ),
        in_specs=[vmem],
        out_specs=(vmem, vmem),
        scratch_shapes=[
            pltpu.VMEM((4, 4, PART, LANES), F32),
            pltpu.VMEM((4, PART, LANES), F32),
            pltpu.SemaphoreType.DMA((4, 4)),
            pltpu.SemaphoreType.DMA((4, 4)),
        ],
        compiler_params=pltpu.CompilerParams(collective_id=1, has_side_effects=True),
        name="sum_terms",
    )(part)


def on_device(inputs, gates, grad_out, doc_lengths, short_filter, long_filter):
    rows = inputs.shape[1]
    filt, in_before, gates_after, cot_after = entry(
        inputs, gates, grad_out, short_filter, long_filter
    )
    grad_inputs, grad_gates, part = compute(
        doc_lengths, filt, inputs, in_before, gates, gates_after, grad_out, cot_after
    )
    scale = 1.0 / math.sqrt(lax.axis_size("fsdp") * lax.axis_size("ctx") * rows)
    short_share, long_share = reduce(part, scale, short_filter.shape, long_filter.shape)
    return grad_inputs, grad_gates, short_share, long_share


def solution(mesh):
    rows = P("fsdp", "ctx", None)
    return jax.shard_map(
        on_device,
        mesh=mesh,
        in_specs=(rows, rows, rows, P("fsdp", None), P(None, "fsdp"), P(None, "fsdp")),
        out_specs=(rows, rows, P(None, "fsdp"), P(None, "fsdp")),
        check_vma=False,
    )
```

time: 802 us -> 126 us (0.16)
  blocking collectives: 378 us -> 0 us
  matrix products: 163 us -> 0 us
  Pallas kernels: 0 us -> 113 us
  waiting for transfers between devices: 82 us -> 0 us
  local copies, waits for them, and re-layouts: 93.2 us -> 12 us
  other arithmetic: 49.8 us -> 0 us
  between operations: 14.7 us -> 0.68 us
  starting transfers between devices: 8.27 us -> 0 us
    psum x1 -> x0, blocking collectives: 358 us -> none  [on_device(): short_whole, long_whole = lax.psum((short_part, long_part), 'ctx')]
    dot_general x24 -> x0, matrix products: 163 us -> none  [the longest x8 115 us: one_block(): jnp.einsum('gst,stk->kg', correlation, picker, precision=lax.Precision.HI...]
    pallas_call x0 -> x3, Pallas kernels: none -> 113 us  [the longest x1 46.5 us: compute(): pl.pallas_call(compute_kernel, grid=(channels // LANES,), out_shape=(jax....]
    unnamed x4 -> x0, waiting for transfers between devices: 80 us -> none
    dynamic_slice x32 -> x0, local copies, waits for them, and re-layouts: 38.7 us -> none  [the longest x8 22.5 us: one_block(): window = lax.dynamic_slice_in_dim(cot_ext, block_start, span_rows, 0)]
    dynamic_update_slice x16 -> x0, local copies, waits for them, and re-layouts: 24.1 us -> none  [long_terms(): lax.map(one_block, jnp.arange(row_count // block_rows, dtype=jnp.int32))]
    all_gather x2 -> x0, blocking collectives: 20 us -> none  [the longest x1 10.3 us: on_device(): lax.all_gather(short_filter, 'fsdp', axis=1, tiled=True)]
    reduce_sum x20 -> x0, other arithmetic: 18.3 us -> none  [the longest x9 17.2 us: short_backward(): jnp.sum(product.reshape(row_count, groups, channels // groups), axis=(0, 2))]
  transfers between devices with their start and end apart: 5 -> 0, of which waited for: 3 -> 0; matrix products, arithmetic and copies ran while one was open for 6% -> 0% of each run, Pallas kernels for 0% -> 0%
where the time goes in v1:
time: 126 us; the launch traced here: 125 us
  Pallas kernels  113 us (90%)
  local copies, waits for them, and re-layouts  12 us (10%)
    pallas_call x1, Pallas kernels, compute(): pl.pallas_call(compute_kernel, grid=(channels // LANES,), out_shape=(jax....  46.5 us
    pallas_call x1, Pallas kernels, entry(): pl.pallas_call(entry_kernel, out_shape=(jax.ShapeDtypeStruct((peers, FILT...  38.9 us
    pallas_call x1, Pallas kernels, reduce(): pl.pallas_call(functools.partial(reduce_kernel, scale), out_shape=(jax.Sh...  27.3 us
    unnamed x21, local copies, waits for them, and re-layouts  12 us

profile of v1, /device:TPU:16, one launch (start us, length us, event | category | flops | bytes accessed | tf_op | source)
XLA Modules:
  0.0 125.5 jit_solution(5079054481869920367)
XLA Ops:
  0.6 1.4 %copy.10.long_ref = bf16[128,64]{1,0:T(8,128)(2,1)} copy(bf16[128,64]{0,1:T(8,128)(2,1)} %param.11) | data formatting | bytes 32768 | tf_op args[5]
  2.1 0.0 copy-start
  2.1 0.0 copy-start.8
  2.1 38.9 %entry.1 = (bf16[4,80,128]{2,1,0:T(8,128)(2,1)}, bf16[16,4096]{1,0:T(8,128)(2,1)}, bf16[16,4096]{1,0:T(8,128)(2,1)}, bf16[144,4096]{1,0:T(8,128)(2,1)}) custom-call(bf16[1,256,4096]{2,1,0:T(8,128)(2,1)} %inputs.3, bf16[1,256,4096]{2,1,0:T(8,128)(2,1)} %gates.3, bf16[1,256,4096]{2,1,0:T(8,128)(2,1)} %cot.3, bf16[7,64]{1,0:T(8,128)(2,1)} %short_ref.1, ...), custom_call_target="tpu_custom_call" | custom-call | tf_op jit(solution)/shard_map/entry/pallas_call | solution.py:91
  41.0 0.0 copy-done
  41.0 0.0 copy-done.8
  41.0 0.0 copy-start.1
  41.0 1.6 %copy-done.1 = bf16[1,256,4096]{2,1,0:T(8,128)(2,1)S(1)} copy-done((bf16[1,256,4096]{2,1,0:T(8,128)(2,1)S(1)}, bf16[1,256,4096]{2,1,0:T(8,128)(2,1)}, u32[]{:S(2)}) %copy-start.1) | copy-done | bytes 2097176
  42.6 0.0 copy-start.2
  42.6 1.6 %copy-done.2 = bf16[1,256,4096]{2,1,0:T(8,128)(2,1)S(1)} copy-done((bf16[1,256,4096]{2,1,0:T(8,128)(2,1)S(1)}, bf16[1,256,4096]{2,1,0:T(8,128)(2,1)}, u32[]{:S(2)}) %copy-start.2) | copy-done | bytes 2097176
  44.2 0.0 copy-start.3
  44.2 1.3 %copy-done.3 = bf16[144,4096]{1,0:T(8,128)(2,1)S(1)} copy-done((bf16[144,4096]{1,0:T(8,128)(2,1)S(1)}, bf16[144,4096]{1,0:T(8,128)(2,1)}, u32[]{:S(2)}) %copy-start.3) | copy-done | bytes 1179672
  45.5 0.0 copy-start.5
  45.5 0.9 copy-done.5
  46.4 0.0 copy-start.6
  46.4 0.9 copy-done.6
  47.3 0.0 copy-start.7
  47.3 0.9 copy-done.7
  48.2 46.5 %layer_pair.1 = (bf16[1,256,4096]{2,1,0:T(8,128)(2,1)}, bf16[1,256,4096]{2,1,0:T(8,128)(2,1)}, f32[4,72,128]{2,1,0:T(8,128)S(1)}) custom-call(s32[1,64]{1,0:T(1,128)S(1)} %copy-done.8, bf16[4,80,128]{2,1,0:T(8,128)(2,1)S(1)} %copy-done.7, bf16[1,256,4096]{2,1,0:T(8,128)(2,1)S(1)} %copy-done, bf16[16,4096]{1,0:T(8,128)(2,1)S(1)} %copy-done.5, ...), custom_call_target="tpu_custom_call" | custom-call | tf_op jit(solution)/shard_map/layer_pair/pallas_call | solution.py:284
  94.7 0.0 copy-start.4
  94.7 0.6 copy-done.4
  95.4 27.3 %sum_terms.1 = (f32[7,64]{1,0:T(8,128)}, f32[128,64]{1,0:T(8,128)}) custom-call(f32[4,72,128]{2,1,0:T(8,128)} %copy-done.4), custom_call_target="tpu_custom_call" | custom-call | tf_op jit(solution)/shard_map/sum_terms/pallas_call | solution.py:383
  122.7 1.5 %copy.11 = f32[128,64]{0,1:T(8,128)} copy(f32[128,64]{1,0:T(8,128)} %get-tuple-element.25) | data formatting | bytes 65536
  124.2 1.3 %copy.13 = f32[7,64]{1,0:T(8,128)} copy(f32[7,64]{1,0:T(8,128)} %get-tuple-element.32) | data formatting | bytes 3584
Async XLA Ops:
  2.1 38.9 %copy-start = (bf16[1,256,4096]{2,1,0:T(8,128)(2,1)S(1)}, bf16[1,256,4096]{2,1,0:T(8,128)(2,1)}, u32[]{:S(2)}) copy-start(bf16[1,256,4096]{2,1,0:T(8,128)(2,1)} %inputs.3) | copy-start | bytes 6291460
  2.1 39.0 %copy-start.8 = (s32[1,64]{1,0:T(1,128)S(1)}, s32[1,64]{1,0:T(1,128)}, u32[]{:S(2)}) copy-start(s32[1,64]{1,0:T(1,128)} %lengths.1) | copy-start | bytes 772
  41.0 1.6 %copy-start.1 = (bf16[1,256,4096]{2,1,0:T(8,128)(2,1)S(1)}, bf16[1,256,4096]{2,1,0:T(8,128)(2,1)}, u32[]{:S(2)}) copy-start(bf16[1,256,4096]{2,1,0:T(8,128)(2,1)} %gates.3) | copy-start | bytes 6291460
  42.6 1.6 %copy-start.2 = (bf16[1,256,4096]{2,1,0:T(8,128)(2,1)S(1)}, bf16[1,256,4096]{2,1,0:T(8,128)(2,1)}, u32[]{:S(2)}) copy-start(bf16[1,256,4096]{2,1,0:T(8,128)(2,1)} %cot.3) | copy-start | bytes 6291460
  44.2 1.3 %copy-start.3 = (bf16[144,4096]{1,0:T(8,128)(2,1)S(1)}, bf16[144,4096]{1,0:T(8,128)(2,1)}, u32[]{:S(2)}) copy-start(bf16[144,4096]{1,0:T(8,128)(2,1)} %get-tuple-element.16.cot_after) | copy-start | bytes 3538948
  45.5 0.9 copy-start.5
  46.4 0.9 copy-start.6
  47.3 0.9 copy-start.7
  94.7 0.7 copy-start.4

commit v2 on v1

v2 whole, which is shorter than its diff:
```python
import functools
import math

import jax
import jax.numpy as jnp
from jax import lax
from jax.experimental import pallas as pl
from jax.experimental.pallas import tpu as pltpu
from jax.sharding import PartitionSpec as P

MESH = pl.DeviceIdType.MESH
F32 = jnp.float32
BF16 = jnp.bfloat16

LANES = 128
TAPS = 128
SHORT = 7
BLOCK = 128
HALO = 144
EXT = 16
WIDTH = 16
PER = LANES // WIDTH
PIECES = 8
FILT = 80
PART = 80


def ring(axis, distance):
    n = lax.axis_size(axis)
    return lax.rem(lax.axis_index(axis) + distance + n, n)


def prepare(lengths, win_mask, ext_mask, diag_mask, fwd_mask, bwd_mask, rcol, row0):
    docs = lengths.shape[1]
    rows = fwd_mask.shape[1]
    lane_pos = row0 + lax.broadcasted_iota(jnp.int32, (8, 512), 1)
    row_pos = row0 + lax.broadcasted_iota(jnp.int32, rcol.shape, 0)

    def one_doc(d, carry):
        end, lane_start, row_start = carry
        end = end + lengths[0, d]
        return (
            end,
            jnp.where(lane_pos >= end, end, lane_start),
            jnp.where(row_pos >= end, end, row_start),
        )

    _, lane_start, row_start = lax.fori_loop(
        0, docs, one_doc,
        (jnp.int32(0), jnp.zeros((8, 512), jnp.int32), jnp.zeros(rcol.shape, jnp.int32)),
    )
    rcol[...] = (row_pos - row_start).astype(F32)
    for j in range(1, SHORT):
        fwd_mask[j - 1] = (rcol[0:rows, :] >= j).astype(F32)
        bwd_mask[j - 1] = (rcol[j : j + rows, :] >= j).astype(F32)
    s_rel = lax.broadcasted_iota(jnp.int32, (BLOCK, LANES), 0)
    lane = lax.broadcasted_iota(jnp.int32, (BLOCK, LANES), 1)
    near = lane >= s_rel
    for b in range(rows // BLOCK):
        s_abs = row0 + b * BLOCK + s_rel
        t0 = jnp.broadcast_to(lane_start[0:1, b * BLOCK : b * BLOCK + LANES], (BLOCK, LANES))
        t1 = jnp.broadcast_to(
            lane_start[0:1, (b + 1) * BLOCK : (b + 1) * BLOCK + LANES], (BLOCK, LANES)
        )
        m0 = jnp.where(near & (t0 <= s_abs), 1.0, 0.0).astype(F32)
        m1 = jnp.where(jnp.logical_not(near) & (t1 <= s_abs), 1.0, 0.0).astype(F32)
        win_mask[b, :, 0:LANES] = m0.astype(BF16)
        win_mask[b, :, LANES:] = m1.astype(BF16)
        diag_mask[b] = m0 + m1
    s_abs = row0 + rows + s_rel[0:EXT]
    t0 = jnp.broadcast_to(lane_start[0:1, rows : rows + LANES], (EXT, LANES))
    t1 = jnp.broadcast_to(lane_start[0:1, rows + LANES : rows + 2 * LANES], (EXT, LANES))
    m0 = jnp.where(near[0:EXT] & (t0 <= s_abs), 1.0, 0.0).astype(F32)
    m1 = jnp.where(jnp.logical_not(near[0:EXT]) & (t1 <= s_abs), 1.0, 0.0).astype(F32)
    ext_mask[:, 0:LANES] = m0.astype(BF16)
    ext_mask[:, LANES:] = m1.astype(BF16)


def chunk(q):
    return pl.ds(pl.multiple_of(q * LANES, LANES), LANES)


def lane_groups(rows):
    return lax.broadcasted_iota(jnp.int32, (rows, LANES), 1) // WIDTH


def chunk_taps(filt32, share, at):
    spread = (
        lax.broadcasted_iota(jnp.int32, (LANES, LANES), 0)
        == at * PER + lax.broadcasted_iota(jnp.int32, (LANES, LANES), 1) // WIDTH
    ).astype(F32)
    return jnp.dot(
        filt32[share, 64:72, :].astype(BF16), spread.astype(BF16), preferred_element_type=F32
    )


def pick(stacked, rows):
    group = lane_groups(rows)
    picked = stacked[0:rows, :]
    for g in range(1, PER):
        picked = jnp.where(group == g, stacked[g * rows : (g + 1) * rows, :], picked)
    return picked


def split_groups(split, gated):
    group = lane_groups(BLOCK)
    for g in range(PER):
        split[g * BLOCK : (g + 1) * BLOCK, :] = jnp.where(group == g, gated, jnp.zeros((), BF16))


def tap_sums(corr, diag):
    lane8 = lax.broadcasted_iota(jnp.int32, (8, LANES), 1)
    row8 = lax.broadcasted_iota(jnp.int32, (8, LANES), 0)
    tap_rows = []
    for g in range(PER):
        total = jnp.zeros((8, LANES), F32)
        for i in range(BLOCK // 8):
            at_row = g * BLOCK + 8 * i
            merged = diag[8 * i : 8 * i + 8, :] * jnp.where(
                lane8 >= row8 + 8 * i,
                corr[at_row : at_row + 8, 0:LANES],
                corr[at_row : at_row + 8, LANES:],
            )
            total = total + (pltpu.roll(merged, LANES - 8 * i, 1) if i else merged)
        for bit in (1, 2, 4):
            total = jnp.where((row8 & bit) > 0, pltpu.roll(total, LANES - bit, 1), total)
        tap_rows.append(jnp.sum(total, axis=0, keepdims=True))
    return jnp.concatenate(tap_rows, axis=0)


def pair_kernel(
    lengths, inputs, gates, cot, short_ref, long_ref,
    gin_out, ggate_out, part_out,
    mine, filt, filt32, x_all, before_all, g_all, cot_all, act_all, ag_all, circ_all,
    win_mask, ext_mask, diag_mask, fwd_mask, bwd_mask, rcol,
    x_s, ag_s, split, table, ext_table, corr, back_all, back_ext,
    own_sem, send_sem, recv_sem, cot_send, cot_recv,
):
    rows, channels = inputs.shape[1:]
    chunks = channels // LANES
    per_share = 64 // PER
    width = channels // PIECES
    peers = lax.axis_size("fsdp")
    f = lax.axis_index("fsdp")
    ctx = lax.axis_index("ctx")
    row0 = ctx * rows
    after, before = ring("ctx", 1), ring("ctx", -1)
    barrier = pltpu.get_barrier_semaphore()
    for to in (after, before):
        pl.semaphore_signal(barrier, inc=1, device_id=(to, f), device_id_type=MESH)
    for d in range(1, peers):
        pl.semaphore_signal(barrier, inc=1, device_id=(ctx, ring("fsdp", d)), device_id_type=MESH)
    local = [
        pltpu.make_async_copy(inputs.at[0], x_all, own_sem.at[0]),
        pltpu.make_async_copy(gates.at[0], g_all.at[pl.ds(0, rows), :], own_sem.at[1]),
        pltpu.make_async_copy(cot.at[0], cot_all.at[pl.ds(0, rows), :], own_sem.at[2]),
    ]
    for c in local:
        c.start()
    mine[...] = jnp.zeros_like(mine)
    mine[0:64, :] = long_ref[...]
    mine[64 : 64 + SHORT, 0:64] = short_ref[...]
    pl.semaphore_wait(barrier, peers + 1)
    small = []
    for d in range(1, peers):
        small.append(
            pltpu.make_async_remote_copy(
                mine, filt.at[f], send_sem.at[d], recv_sem.at[d],
                device_id=(ctx, ring("fsdp", d)), device_id_type=MESH,
            )
        )
    small.append(
        pltpu.make_async_remote_copy(
            inputs.at[0, pl.ds(rows - 16, 16), :], before_all, send_sem.at[4], recv_sem.at[4],
            device_id=(after, f), device_id_type=MESH,
        )
    )
    for c in small:
        c.start()

    def piece(p):
        lanes = pl.ds(pl.multiple_of(p * width, LANES), width)
        return pltpu.make_async_remote_copy(
            cot.at[0, pl.ds(0, HALO), lanes], cot_all.at[pl.ds(rows, HALO), lanes],
            cot_send.at[p], cot_recv.at[p],
            device_id=(before, f), device_id_type=MESH,
        )

    gate_copy = pltpu.make_async_remote_copy(
        gates.at[0, pl.ds(0, EXT), :], g_all.at[pl.ds(rows, EXT), :],
        send_sem.at[5], recv_sem.at[5],
        device_id=(before, f), device_id_type=MESH,
    )
    gate_copy.start()
    for p in range(PIECES):
        piece(p).start()

    prepare(lengths, win_mask, ext_mask, diag_mask, fwd_mask, bwd_mask, rcol, row0)
    cot_all[rows + HALO :, :] = jnp.zeros((cot_all.shape[0] - rows - HALO, channels), BF16)
    part_out[...] = jnp.zeros_like(part_out)
    filt[f] = mine[...]
    for c in small:
        c.wait_recv()
    for c in local:
        c.wait()
    filt32[...] = filt[...].astype(F32)

    def first_half(q, carry):
        lanes = chunk(q)
        share, at = q // per_share, lax.rem(q, per_share)
        taps = chunk_taps(filt32, share, at)
        own_groups = pl.ds(pl.multiple_of(at * PER, PER), PER)
        long_rows = filt32[share, own_groups, :]
        x_s[0:8, :] = before_all[:, lanes].astype(F32)[8:16]
        x_s[8:, :] = x_all[:, lanes].astype(F32)
        act = taps[0:1, :] * x_s[8 : 8 + rows, :]
        for j in range(1, SHORT):
            act = act + fwd_mask[j - 1] * (taps[j : j + 1, :] * x_s[8 - j : 8 - j + rows, :])
        act = act.astype(BF16)
        act_all[:, lanes] = act
        act = act[0:BLOCK].astype(F32)
        gate = g_all[0:BLOCK, lanes].astype(F32)
        split_groups(split, (gate * act).astype(BF16))
        for g in range(PER):
            circ = pltpu.roll(
                jnp.broadcast_to(long_rows[g : g + 1, :], (BLOCK, LANES)), 0, 1,
                stride=1, stride_axis=0,
            ).astype(BF16)
            circ_all[q, g * BLOCK : (g + 1) * BLOCK, :] = circ
            table[g * BLOCK : (g + 1) * BLOCK, 0:LANES] = circ * win_mask[0, :, 0:LANES]
            table[g * BLOCK : (g + 1) * BLOCK, LANES:] = circ * win_mask[0, :, LANES:]
        window = cot_all[0 : 2 * BLOCK, lanes]
        corr[...] = lax.dot_general(
            split[...], window, (((1,), (1,)), ((), ())), preferred_element_type=F32
        )
        back_all[...] = jnp.dot(table[...], window, preferred_element_type=F32)
        part_out[share, own_groups, :] = tap_sums(corr, diag_mask.at[0])
        back = pick(back_all, BLOCK)
        ag_all[:, lanes] = (back * gate).astype(BF16)
        ggate_out[0, 0:BLOCK, lanes] = (back * act).astype(BF16)
        return carry

    lax.fori_loop(0, chunks, first_half, 0)
    gate_copy.wait_recv()

    def second_half(q):
        lanes = chunk(q)
        share, at = q // per_share, lax.rem(q, per_share)
        taps = chunk_taps(filt32, share, at)
        own_groups = pl.ds(pl.multiple_of(at * PER, PER), PER)
        gate = g_all[BLOCK:, lanes].astype(F32)
        act = act_all[BLOCK:, lanes].astype(F32)
        split_groups(split, (gate[0:BLOCK] * act).astype(BF16))
        for g in range(PER):
            circ = circ_all[q, g * BLOCK : (g + 1) * BLOCK, :]
            table[g * BLOCK : (g + 1) * BLOCK, 0:LANES] = circ * win_mask[1, :, 0:LANES]
            table[g * BLOCK : (g + 1) * BLOCK, LANES:] = circ * win_mask[1, :, LANES:]
            ext_table[g * EXT : (g + 1) * EXT, 0:LANES] = circ[0:EXT] * ext_mask[:, 0:LANES]
            ext_table[g * EXT : (g + 1) * EXT, LANES:] = circ[0:EXT] * ext_mask[:, LANES:]
        window = cot_all[BLOCK : 3 * BLOCK, lanes]
        corr[...] = lax.dot_general(
            split[...], window, (((1,), (1,)), ((), ())), preferred_element_type=F32
        )
        back_all[...] = jnp.dot(table[...], window, preferred_element_type=F32)
        back_ext[...] = jnp.dot(
            ext_table[...], cot_all[2 * BLOCK : 4 * BLOCK, lanes], preferred_element_type=F32
        )
        part_out[share, own_groups, :] += tap_sums(corr, diag_mask.at[1])
        back = pick(back_all, BLOCK)
        ag_s[0:BLOCK, :] = ag_all[:, lanes].astype(F32)
        ag_s[BLOCK:rows, :] = (back * gate[0:BLOCK]).astype(BF16).astype(F32)
        ag_s[rows:, :] = (pick(back_ext, EXT) * gate[BLOCK:]).astype(BF16).astype(F32)
        ggate_out[0, BLOCK:, lanes] = (back * act).astype(BF16)

        x = x_all[:, lanes].astype(F32)
        gin = jnp.zeros((rows, LANES), F32)
        terms = []
        for j in range(SHORT):
            moved = ag_s[j : j + rows, :]
            if j:
                moved = bwd_mask[j - 1] * moved
            gin = gin + taps[j : j + 1, :] * moved
            terms.append(jnp.sum(moved * x, axis=0, keepdims=True))
        gin_out[0, :, lanes] = gin.astype(BF16)
        terms.append(jnp.zeros((1, LANES), F32))
        gathered = (
            lax.broadcasted_iota(jnp.int32, (LANES, LANES), 1)
            == at * PER + lax.broadcasted_iota(jnp.int32, (LANES, LANES), 0) // WIDTH
        ).astype(F32)
        part_out[share, 64:72, :] += jnp.dot(
            jnp.concatenate(terms, axis=0), gathered,
            preferred_element_type=F32, precision=lax.Precision.HIGHEST,
        )

    def one_piece(p, carry):
        piece(p).wait_recv()

        def inner(i, c):
            second_half(p * (chunks // PIECES) + i)
            return c

        return lax.fori_loop(0, chunks // PIECES, inner, carry)

    lax.fori_loop(0, PIECES, one_piece, 0)
    for c in small:
        c.wait_send()
    gate_copy.wait_send()
    for p in range(PIECES):
        piece(p).wait_send()


def layer_pair(inputs, gates, cot, lengths, short_filter, long_filter):
    _, rows, channels = inputs.shape
    assert rows == 2 * BLOCK
    shares = lax.axis_size("fsdp")
    chunks = channels // LANES
    anyspace = pl.BlockSpec(memory_space=pl.ANY)
    vmem = pl.BlockSpec(memory_space=pltpu.VMEM)
    stack = PER * BLOCK
    return pl.pallas_call(
        pair_kernel,
        out_shape=(
            jax.ShapeDtypeStruct(inputs.shape, BF16),
            jax.ShapeDtypeStruct(inputs.shape, BF16),
            jax.ShapeDtypeStruct((shares, PART, LANES), F32),
        ),
        in_specs=[pl.BlockSpec(memory_space=pltpu.SMEM), anyspace, anyspace, anyspace, vmem, vmem],
        out_specs=(vmem, vmem, vmem),
        scratch_shapes=[
            pltpu.VMEM((FILT, LANES), BF16),
            pltpu.VMEM((shares, FILT, LANES), BF16),
            pltpu.VMEM((shares, FILT, LANES), F32),
            pltpu.VMEM((rows, channels), BF16),
            pltpu.VMEM((16, channels), BF16),
            pltpu.VMEM((rows + EXT, channels), BF16),
            pltpu.VMEM((rows + 2 * BLOCK, channels), BF16),
            pltpu.VMEM((rows, channels), BF16),
            pltpu.VMEM((BLOCK, channels), BF16),
            pltpu.VMEM((chunks, stack, LANES), BF16),
            pltpu.VMEM((2, BLOCK, 2 * LANES), BF16),
            pltpu.VMEM((EXT, 2 * LANES), BF16),
            pltpu.VMEM((2, BLOCK, LANES), F32),
            pltpu.VMEM((SHORT - 1, rows, LANES), F32),
            pltpu.VMEM((SHORT - 1, rows, LANES), F32),
            pltpu.VMEM((rows + EXT, LANES), F32),
            pltpu.VMEM((rows + 8, LANES), F32),
            pltpu.VMEM((rows + EXT, LANES), F32),
            pltpu.VMEM((stack, LANES), BF16),
            pltpu.VMEM((stack, 2 * LANES), BF16),
            pltpu.VMEM((PER * EXT, 2 * LANES), BF16),
            pltpu.VMEM((stack, 2 * LANES), F32),
            pltpu.VMEM((stack, LANES), F32),
            pltpu.VMEM((PER * EXT, LANES), F32),
            pltpu.SemaphoreType.DMA((3,)),
            pltpu.SemaphoreType.DMA((6,)),
            pltpu.SemaphoreType.DMA((6,)),
            pltpu.SemaphoreType.DMA((PIECES,)),
            pltpu.SemaphoreType.DMA((PIECES,)),
        ],
        compiler_params=pltpu.CompilerParams(
            collective_id=0, has_side_effects=True, vmem_limit_bytes=56 << 20
        ),
        name="layer_pair",
    )(lengths, inputs, gates, cot, short_filter, long_filter)


def reduce_kernel(scale, part, short_out, long_out, half, landed, bufs, cur, send_sem, recv_sem):
    side = 4
    f = lax.axis_index("fsdp")
    ctx = lax.axis_index("ctx")
    core, high = lax.rem(f, 2), f // 2
    y, low, x = lax.rem(ctx, side), lax.rem(ctx // side, side), ctx // (side * side)
    core_peer = (ctx, high * 2 + 1 - core)
    high_peer = (ctx, (1 - high) * 2 + core)
    axes = ((y, 1), (x, side * side), (low, side))

    def peer(axis, d):
        at, stride = axes[axis]
        return (ctx + (lax.rem(at + d, side) - at) * stride, f)

    barrier = pltpu.get_barrier_semaphore()
    for to in [core_peer, high_peer] + [peer(a, d) for a in range(3) for d in range(1, side)]:
        pl.semaphore_signal(barrier, inc=1, device_id=to, device_id_type=MESH)
    pl.semaphore_wait(barrier, 2 + 3 * (side - 1))

    swaps = [
        pltpu.make_async_remote_copy(
            part.at[2 * h + 1 - core], half.at[h], send_sem.at[0, h], recv_sem.at[0, h],
            device_id=core_peer, device_id_type=MESH,
        )
        for h in range(2)
    ]
    for c in swaps:
        c.start()
    for c in swaps:
        c.wait_recv()
    cur[0] = (part[2 * (1 - high) + core] + half[1 - high]).astype(BF16)
    cross = pltpu.make_async_remote_copy(
        cur.at[0], landed, send_sem.at[1, 0], recv_sem.at[1, 0],
        device_id=high_peer, device_id_type=MESH,
    )
    cross.start()
    total = part[2 * high + core] + half[high]
    cross.wait_recv()
    total = total + landed[...].astype(F32)
    sent = swaps + [cross]
    for axis in range(3):
        at = axes[axis][0]
        cur[axis + 1] = total.astype(BF16)
        copies = [
            pltpu.make_async_remote_copy(
                cur.at[axis + 1], bufs.at[axis, side - d],
                send_sem.at[axis + 2, d], recv_sem.at[axis + 2, side - d],
                device_id=peer(axis, d), device_id_type=MESH,
            )
            for d in range(1, side)
        ]
        for c in copies:
            c.start()
        sent += copies
        bufs[axis, 0] = cur[axis + 1]
        for c in copies:
            c.wait_recv()
        total = jnp.zeros(total.shape, F32)
        for place in range(side):
            total = total + bufs[axis, lax.rem(place - at + side, side)].astype(F32)
    total = total * scale
    long_out[...] = total[0:64]
    short_out[...] = total[64 : 64 + SHORT, 0:64]
    for c in sent:
        c.wait_send()


def reduce(part, scale, short_shape, long_shape):
    vmem = pl.BlockSpec(memory_space=pltpu.VMEM)
    return pl.pallas_call(
        functools.partial(reduce_kernel, scale),
        out_shape=(
            jax.ShapeDtypeStruct(short_shape, F32),
            jax.ShapeDtypeStruct(long_shape, F32),
        ),
        in_specs=[vmem],
        out_specs=(vmem, vmem),
        scratch_shapes=[
            pltpu.VMEM((2, PART, LANES), F32),
            pltpu.VMEM((PART, LANES), BF16),
            pltpu.VMEM((3, 4, PART, LANES), BF16),
            pltpu.VMEM((4, PART, LANES), BF16),
            pltpu.SemaphoreType.DMA((5, 4)),
            pltpu.SemaphoreType.DMA((5, 4)),
        ],
        compiler_params=pltpu.CompilerParams(collective_id=1, has_side_effects=True),
        name="sum_terms",
    )(part)


def on_device(inputs, gates, grad_out, doc_lengths, short_filter, long_filter):
    rows = inputs.shape[1]
    grad_inputs, grad_gates, part = layer_pair(
        inputs, gates, grad_out, doc_lengths, short_filter, jnp.transpose(long_filter)
    )
    scale = 1.0 / math.sqrt(lax.axis_size("fsdp") * lax.axis_size("ctx") * rows)
    short_share, long_share = reduce(part, scale, short_filter.shape, long_filter.shape[::-1])
    return grad_inputs, grad_gates, short_share, jnp.transpose(long_share)


def solution(mesh):
    rows = P("fsdp", "ctx", None)
    return jax.shard_map(
        on_device,
        mesh=mesh,
        in_specs=(rows, rows, rows, P("fsdp", None), P(None, "fsdp"), P(None, "fsdp")),
        out_specs=(rows, rows, P(None, "fsdp"), P(None, "fsdp")),
        check_vma=False,
    )
```

time: 126 us -> 104 us (0.83)
  Pallas kernels: 113 us -> 97.7 us
  local copies, waits for them, and re-layouts: 12 us -> 5.82 us
    pallas_call x2 -> x1, Pallas kernels: 85.5 us -> 72 us  [layer_pair(): pl.pallas_call(pair_kernel, out_shape=(jax.ShapeDtypeStruct(inputs.shape,...]
    unnamed x21 -> x10, local copies, waits for them, and re-layouts: 12 us -> 5.82 us
    pallas_call x1, Pallas kernels: 27.3 us -> 25.7 us  [reduce(): pl.pallas_call(functools.partial(reduce_kernel, scale), out_shape=(jax.Sh...]
where the time goes in v2:
time: 104 us
  Pallas kernels  97.7 us (94%)
  local copies, waits for them, and re-layouts  5.82 us (6%)
    pallas_call x1, Pallas kernels, layer_pair(): pl.pallas_call(pair_kernel, out_shape=(jax.ShapeDtypeStruct(inputs.shape,...  72 us
    pallas_call x1, Pallas kernels, reduce(): pl.pallas_call(functools.partial(reduce_kernel, scale), out_shape=(jax.Sh...  25.7 us
    unnamed x10, local copies, waits for them, and re-layouts  5.82 us

profile of v2, /device:TPU:16, one launch (start us, length us, event | category | flops | bytes accessed | tf_op | source)
XLA Modules:
  0.0 104.2 jit_solution(18413832958511736773)
XLA Ops:
  0.6 72.0 %layer_pair.1 = (bf16[1,256,4096]{2,1,0:T(8,128)(2,1)}, bf16[1,256,4096]{2,1,0:T(8,128)(2,1)}, f32[4,80,128]{2,1,0:T(8,128)}) custom-call(s32[1,64]{1,0:T(1,128)} %lengths.1, bf16[1,256,4096]{2,1,0:T(8,128)(2,1)} %inputs.1, bf16[1,256,4096]{2,1,0:T(8,128)(2,1)} %gates.1, bf16[1,256,4096]{2,1,0:T(8,128)(2,1)} %cot.1, bf16[7,64]{1,0:T(8,128)(2,1)} %short_ref.1, ...), custom_call_target="tpu_custom_call" | custom-call | tf_op jit(solution)/shard_map/layer_pair/pallas_call | solution.py:320
  72.7 25.7 %sum_terms.1 = (f32[7,64]{1,0:T(8,128)}, f32[64,128]{1,0:T(8,128)}) custom-call(f32[4,80,128]{2,1,0:T(8,128)} %get-tuple-element.11.part), custom_call_target="tpu_custom_call" | custom-call | tf_op jit(solution)/shard_map/sum_terms/pallas_call | solution.py:436
  98.4 0.0 copy-start
  98.4 3.3 %copy.14 = bf16[1,256,4096]{2,1,0:T(8,128)(2,1)} copy(bf16[1,256,4096]{2,1,0:T(8,128)(2,1)} %get-tuple-element.18) | data formatting | bytes 4194304
  101.7 0.0 copy-done
  101.7 0.0 copy-start.2
  101.7 0.0 copy-start.1
  101.7 1.3 %copy.15 = bf16[1,256,4096]{2,1,0:T(8,128)(2,1)} copy(bf16[1,256,4096]{2,1,0:T(8,128)(2,1)S(1)} %copy-done) | data formatting | bytes 4194304
  103.0 0.0 copy-done.2
  103.0 0.6 copy.16
  103.6 0.0 copy-done.1
  103.6 0.6 copy.17
Async XLA Ops:
  98.4 3.3 %copy-start = (bf16[1,256,4096]{2,1,0:T(8,128)(2,1)S(1)}, bf16[1,256,4096]{2,1,0:T(8,128)(2,1)}, u32[]{:S(2)}) copy-start(bf16[1,256,4096]{2,1,0:T(8,128)(2,1)} %get-tuple-element.19) | copy-start | bytes 6291460
  101.7 1.3 %copy-start.2 = (f32[7,64]{1,0:T(8,128)S(1)}, f32[7,64]{1,0:T(8,128)}, u32[]{:S(2)}) copy-start(f32[7,64]{1,0:T(8,128)} %get-tuple-element.20) | copy-start | bytes 5380
  101.7 1.9 %copy-start.1 = (f32[64,128]{1,0:T(8,128)S(1)}, f32[64,128]{1,0:T(8,128)}, u32[]{:S(2)}) copy-start(f32[64,128]{1,0:T(8,128)} %get-tuple-element.13) | copy-start | bytes 98308

commit v3 on v2

--- a/solution.py
+++ b/solution.py
@@ -16,10 +16,12 @@
 TAPS = 128
 SHORT = 7
 BLOCK = 128
+SUB = 32
 HALO = 144
 EXT = 16
 WIDTH = 16
 PER = LANES // WIDTH
+PARTS = 4
 PIECES = 8
 FILT = 80
 PART = 80
@@ -34,44 +36,45 @@
     docs = lengths.shape[1]
     rows = fwd_mask.shape[1]
     lane_pos = row0 + lax.broadcasted_iota(jnp.int32, (8, 512), 1)
-    row_pos = row0 + lax.broadcasted_iota(jnp.int32, rcol.shape, 0)
 
     def one_doc(d, carry):
-        end, lane_start, row_start = carry
+        end, start = carry
         end = end + lengths[0, d]
-        return (
-            end,
-            jnp.where(lane_pos >= end, end, lane_start),
-            jnp.where(row_pos >= end, end, row_start),
-        )
-
-    _, lane_start, row_start = lax.fori_loop(
-        0, docs, one_doc,
-        (jnp.int32(0), jnp.zeros((8, 512), jnp.int32), jnp.zeros(rcol.shape, jnp.int32)),
-    )
-    rcol[...] = (row_pos - row_start).astype(F32)
+        return end, jnp.where(lane_pos >= end, end, start)
+
+    _, start = lax.fori_loop(0, docs, one_doc, (jnp.int32(0), jnp.zeros((8, 512), jnp.int32)))
+    passed = (lane_pos - start).astype(F32)
+    for k in range(3):
+        own = slice(k * LANES, (k + 1) * LANES)
+        turned = jnp.transpose(jnp.broadcast_to(passed[0:1, own], (LANES, LANES)))
+        rcol[k * LANES : k * LANES + LANES, :] = turned
     for j in range(1, SHORT):
         fwd_mask[j - 1] = (rcol[0:rows, :] >= j).astype(F32)
         bwd_mask[j - 1] = (rcol[j : j + rows, :] >= j).astype(F32)
     s_rel = lax.broadcasted_iota(jnp.int32, (BLOCK, LANES), 0)
     lane = lax.broadcasted_iota(jnp.int32, (BLOCK, LANES), 1)
-    near = lane >= s_rel
+
+    def starts_at(first, count):
+        return jnp.broadcast_to(start[0:1, first : first + LANES], (count, LANES))
+
     for b in range(rows // BLOCK):
         s_abs = row0 + b * BLOCK + s_rel
-        t0 = jnp.broadcast_to(lane_start[0:1, b * BLOCK : b * BLOCK + LANES], (BLOCK, LANES))
-        t1 = jnp.broadcast_to(
-            lane_start[0:1, (b + 1) * BLOCK : (b + 1) * BLOCK + LANES], (BLOCK, LANES)
-        )
-        m0 = jnp.where(near & (t0 <= s_abs), 1.0, 0.0).astype(F32)
-        m1 = jnp.where(jnp.logical_not(near) & (t1 <= s_abs), 1.0, 0.0).astype(F32)
+        near = lane >= s_rel
+        first = b * BLOCK
+        m0 = jnp.where(near & (starts_at(first, BLOCK) <= s_abs), 1.0, 0.0)
+        m1 = jnp.where(near | (starts_at(first + LANES, BLOCK) > s_abs), 0.0, 1.0)
         win_mask[b, :, 0:LANES] = m0.astype(BF16)
         win_mask[b, :, LANES:] = m1.astype(BF16)
-        diag_mask[b] = m0 + m1
+        for k in range(BLOCK // SUB):
+            own = slice(k * SUB, (k + 1) * SUB)
+            first = b * BLOCK + k * SUB
+            near = lane[0:SUB] >= s_rel[0:SUB]
+            target = jnp.where(near, starts_at(first, SUB), starts_at(first + LANES, SUB))
+            diag_mask[b, own, :] = jnp.where(target <= s_abs[own], 1.0, 0.0)
     s_abs = row0 + rows + s_rel[0:EXT]
-    t0 = jnp.broadcast_to(lane_start[0:1, rows : rows + LANES], (EXT, LANES))
-    t1 = jnp.broadcast_to(lane_start[0:1, rows + LANES : rows + 2 * LANES], (EXT, LANES))
-    m0 = jnp.where(near[0:EXT] & (t0 <= s_abs), 1.0, 0.0).astype(F32)
-    m1 = jnp.where(jnp.logical_not(near[0:EXT]) & (t1 <= s_abs), 1.0, 0.0).astype(F32)
+    near = (lane >= s_rel)[0:EXT]
+    m0 = jnp.where(near & (starts_at(rows, EXT) <= s_abs), 1.0, 0.0)
+    m1 = jnp.where(near | (starts_at(rows + LANES, EXT) > s_abs), 0.0, 1.0)
     ext_mask[:, 0:LANES] = m0.astype(BF16)
     ext_mask[:, LANES:] = m1.astype(BF16)
 
@@ -94,34 +97,58 @@
     )
 
 
-def pick(stacked, rows):
-    group = lane_groups(rows)
-    picked = stacked[0:rows, :]
+def pick(stacked, first, count, stride):
+    group = lane_groups(count)
+    picked = stacked[first : first + count, :]
     for g in range(1, PER):
-        picked = jnp.where(group == g, stacked[g * rows : (g + 1) * rows, :], picked)
+        at = g * stride + first
+        picked = jnp.where(group == g, stacked[at : at + count, :], picked)
     return picked
 
 
 def split_groups(split, gated):
-    group = lane_groups(BLOCK)
+    group = lane_groups(SUB)
+    for k in range(BLOCK // SUB):
+        for g in range(PER):
+            at = (k * PER + g) * SUB
+            split[at : at + SUB, :] = jnp.where(
+                group == g, gated[k * SUB : (k + 1) * SUB, :], jnp.zeros((), BF16)
+            )
+
+
+def correlate(corr, split, cot_all, first, lanes, k):
+    own = slice(k * PER * SUB, (k + 1) * PER * SUB)
+    reach = SUB + TAPS
+    window = cot_all[first + k * SUB : first + k * SUB + reach, lanes]
+    corr[own, 0:reach] = lax.dot_general(
+        split[own, :], window, (((1,), (1,)), ((), ())), preferred_element_type=F32
+    )
+
+
+def merge(merged, corr, diag):
+    lane8 = lax.broadcasted_iota(jnp.int32, (8, LANES), 1)
+    row8 = lax.broadcasted_iota(jnp.int32, (8, LANES), 0)
     for g in range(PER):
-        split[g * BLOCK : (g + 1) * BLOCK, :] = jnp.where(group == g, gated, jnp.zeros((), BF16))
-
-
-def tap_sums(corr, diag):
-    lane8 = lax.broadcasted_iota(jnp.int32, (8, LANES), 1)
+        for i in range(SUB // 8):
+            total = jnp.zeros((8, LANES), F32)
+            for k in range(BLOCK // SUB):
+                at_row = (k * PER + g) * SUB + 8 * i
+                total = total + diag[k * SUB + 8 * i : k * SUB + 8 * i + 8, :] * jnp.where(
+                    lane8 >= row8 + 8 * i,
+                    corr[at_row : at_row + 8, 0:LANES],
+                    corr[at_row : at_row + 8, LANES:],
+                )
+            merged[g * SUB + 8 * i : g * SUB + 8 * i + 8, :] = total
+
+
+def line_up(merged):
     row8 = lax.broadcasted_iota(jnp.int32, (8, LANES), 0)
     tap_rows = []
     for g in range(PER):
-        total = jnp.zeros((8, LANES), F32)
-        for i in range(BLOCK // 8):
-            at_row = g * BLOCK + 8 * i
-            merged = diag[8 * i : 8 * i + 8, :] * jnp.where(
-                lane8 >= row8 + 8 * i,
-                corr[at_row : at_row + 8, 0:LANES],
-                corr[at_row : at_row + 8, LANES:],
-            )
-            total = total + (pltpu.roll(merged, LANES - 8 * i, 1) if i else merged)
+        total = merged[g * SUB : g * SUB + 8, :]
+        for i in range(1, SUB // 8):
+            at = g * SUB + 8 * i
+            total = total + pltpu.roll(merged[at : at + 8, :], LANES - 8 * i, 1)
         for bit in (1, 2, 4):
             total = jnp.where((row8 & bit) > 0, pltpu.roll(total, LANES - bit, 1), total)
         tap_rows.append(jnp.sum(total, axis=0, keepdims=True))
@@ -133,7 +160,7 @@
     gin_out, ggate_out, part_out,
     mine, filt, filt32, x_all, before_all, g_all, cot_all, act_all, ag_all, circ_all,
     win_mask, ext_mask, diag_mask, fwd_mask, bwd_mask, rcol,
-    x_s, ag_s, split, table, ext_table, corr, back_all, back_ext,
+    x_s, act_next, act_s, terms, merged, ag_s, split, table, ext_table, corr, back_all, back_ext,
     own_sem, send_sem, recv_sem, cot_send, cot_recv,
 ):
     rows, channels = inputs.shape[1:]
@@ -205,92 +232,150 @@
         c.wait()
     filt32[...] = filt[...].astype(F32)
 
+    def place(q):
+        share, at = q // per_share, lax.rem(q, per_share)
+        return share, at, pl.ds(pl.multiple_of(at * PER, PER), PER)
+
+    def load_next(q):
+        lanes = chunk(q)
+        x_s[0:8, :] = before_all[:, lanes].astype(F32)[8:16]
+        x_s[8:, :] = x_all[:, lanes].astype(F32)
+
+    def forward(q, taps, part):
+        lanes = chunk(q)
+        size = rows // PARTS
+        own = slice(part * size, (part + 1) * size)
+        act = taps[0:1, :] * x_s[8 + part * size : 8 + (part + 1) * size, :]
+        for j in range(1, SHORT):
+            at = 8 - j + part * size
+            act = act + fwd_mask[j - 1, own, :] * (taps[j : j + 1, :] * x_s[at : at + size, :])
+        act = act.astype(BF16)
+        act_all[own, lanes] = act
+        if (part + 1) * size <= BLOCK:
+            act_next[own, :] = act.astype(F32)
+
+    def taps_of(q):
+        share, at, _ = place(q)
+        return chunk_taps(filt32, share, at)
+
+    def add_taps(q):
+        share, _, own_groups = place(q)
+        part_out[share, own_groups, :] += line_up(merged)
+
+    merged[...] = jnp.zeros_like(merged)
+    load_next(0)
+    for part in range(PARTS):
+        forward(0, taps_of(0), part)
+
     def first_half(q, carry):
         lanes = chunk(q)
-        share, at = q // per_share, lax.rem(q, per_share)
-        taps = chunk_taps(filt32, share, at)
-        own_groups = pl.ds(pl.multiple_of(at * PER, PER), PER)
+        share, at, own_groups = place(q)
         long_rows = filt32[share, own_groups, :]
-        x_s[0:8, :] = before_all[:, lanes].astype(F32)[8:16]
-        x_s[8:, :] = x_all[:, lanes].astype(F32)
-        act = taps[0:1, :] * x_s[8 : 8 + rows, :]
-        for j in range(1, SHORT):
-            act = act + fwd_mask[j - 1] * (taps[j : j + 1, :] * x_s[8 - j : 8 - j + rows, :])
-        act = act.astype(BF16)
-        act_all[:, lanes] = act
-        act = act[0:BLOCK].astype(F32)
+        add_taps(lax.rem(q + chunks - 1, chunks))
         gate = g_all[0:BLOCK, lanes].astype(F32)
+        act = act_next[...]
+        act_s[...] = act
         split_groups(split, (gate * act).astype(BF16))
-        for g in range(PER):
-            circ = pltpu.roll(
-                jnp.broadcast_to(long_rows[g : g + 1, :], (BLOCK, LANES)), 0, 1,
-                stride=1, stride_axis=0,
-            ).astype(BF16)
-            circ_all[q, g * BLOCK : (g + 1) * BLOCK, :] = circ
-            table[g * BLOCK : (g + 1) * BLOCK, 0:LANES] = circ * win_mask[0, :, 0:LANES]
-            table[g * BLOCK : (g + 1) * BLOCK, LANES:] = circ * win_mask[0, :, LANES:]
+        later = jnp.minimum(q + 1, chunks - 1)
+        taps = taps_of(later)
+        load_next(later)
         window = cot_all[0 : 2 * BLOCK, lanes]
-        corr[...] = lax.dot_general(
-            split[...], window, (((1,), (1,)), ((), ())), preferred_element_type=F32
-        )
-        back_all[...] = jnp.dot(table[...], window, preferred_element_type=F32)
-        part_out[share, own_groups, :] = tap_sums(corr, diag_mask.at[0])
-        back = pick(back_all, BLOCK)
-        ag_all[:, lanes] = (back * gate).astype(BF16)
-        ggate_out[0, 0:BLOCK, lanes] = (back * act).astype(BF16)
+        for part in range(PARTS):
+            for g in range(part * PER // PARTS, (part + 1) * PER // PARTS):
+                own = slice(g * BLOCK, (g + 1) * BLOCK)
+                circ = pltpu.roll(
+                    jnp.broadcast_to(long_rows[g : g + 1, :], (BLOCK, LANES)), 0, 1,
+                    stride=1, stride_axis=0,
+                ).astype(BF16)
+                circ_all[q, own, :] = circ
+                table[own, 0:LANES] = circ * win_mask[0, :, 0:LANES]
+                table[own, LANES:] = circ * win_mask[0, :, LANES:]
+            correlate(corr, split, cot_all, 0, lanes, part)
+            own = slice(part * PER // PARTS * BLOCK, (part + 1) * PER // PARTS * BLOCK)
+            back_all[own, :] = jnp.dot(table[own, :], window, preferred_element_type=F32)
+            forward(later, taps, part)
+        merge(merged, corr, diag_mask.at[0])
+        for part in range(PARTS):
+            own = slice(part * SUB, (part + 1) * SUB)
+            back = pick(back_all, part * SUB, SUB, BLOCK)
+            ag_all[own, lanes] = (back * g_all[own, lanes].astype(F32)).astype(BF16)
+            ggate_out[0, own, lanes] = (back * act_s[own, :]).astype(BF16)
         return carry
 
     lax.fori_loop(0, chunks, first_half, 0)
     gate_copy.wait_recv()
 
-    def second_half(q):
+    ag_s[...] = jnp.zeros_like(ag_s)
+
+    def short_back(q, taps, part):
         lanes = chunk(q)
-        share, at = q // per_share, lax.rem(q, per_share)
-        taps = chunk_taps(filt32, share, at)
-        own_groups = pl.ds(pl.multiple_of(at * PER, PER), PER)
-        gate = g_all[BLOCK:, lanes].astype(F32)
-        act = act_all[BLOCK:, lanes].astype(F32)
-        split_groups(split, (gate[0:BLOCK] * act).astype(BF16))
-        for g in range(PER):
-            circ = circ_all[q, g * BLOCK : (g + 1) * BLOCK, :]
-            table[g * BLOCK : (g + 1) * BLOCK, 0:LANES] = circ * win_mask[1, :, 0:LANES]
-            table[g * BLOCK : (g + 1) * BLOCK, LANES:] = circ * win_mask[1, :, LANES:]
-            ext_table[g * EXT : (g + 1) * EXT, 0:LANES] = circ[0:EXT] * ext_mask[:, 0:LANES]
-            ext_table[g * EXT : (g + 1) * EXT, LANES:] = circ[0:EXT] * ext_mask[:, LANES:]
-        window = cot_all[BLOCK : 3 * BLOCK, lanes]
-        corr[...] = lax.dot_general(
-            split[...], window, (((1,), (1,)), ((), ())), preferred_element_type=F32
-        )
-        back_all[...] = jnp.dot(table[...], window, preferred_element_type=F32)
-        back_ext[...] = jnp.dot(
-            ext_table[...], cot_all[2 * BLOCK : 4 * BLOCK, lanes], preferred_element_type=F32
-        )
-        part_out[share, own_groups, :] += tap_sums(corr, diag_mask.at[1])
-        back = pick(back_all, BLOCK)
-        ag_s[0:BLOCK, :] = ag_all[:, lanes].astype(F32)
-        ag_s[BLOCK:rows, :] = (back * gate[0:BLOCK]).astype(BF16).astype(F32)
-        ag_s[rows:, :] = (pick(back_ext, EXT) * gate[BLOCK:]).astype(BF16).astype(F32)
-        ggate_out[0, BLOCK:, lanes] = (back * act).astype(BF16)
-
-        x = x_all[:, lanes].astype(F32)
-        gin = jnp.zeros((rows, LANES), F32)
-        terms = []
+        size = rows // PARTS
+        first = part * size
+        own = slice(first, first + size)
+        x = x_all[own, lanes].astype(F32)
+        gin = jnp.zeros((size, LANES), F32)
         for j in range(SHORT):
-            moved = ag_s[j : j + rows, :]
+            moved = ag_s[first + j : first + j + size, :]
             if j:
-                moved = bwd_mask[j - 1] * moved
+                moved = bwd_mask[j - 1, own, :] * moved
             gin = gin + taps[j : j + 1, :] * moved
-            terms.append(jnp.sum(moved * x, axis=0, keepdims=True))
-        gin_out[0, :, lanes] = gin.astype(BF16)
-        terms.append(jnp.zeros((1, LANES), F32))
+            product = jnp.sum((moved * x).reshape(size // 8, 8, LANES), axis=0)
+            if part:
+                product = product + terms[8 * j : 8 * j + 8, :]
+            terms[8 * j : 8 * j + 8, :] = product
+        gin_out[0, own, lanes] = gin.astype(BF16)
+
+    def short_terms(q):
+        share, at, _ = place(q)
+        sums = [
+            jnp.sum(terms[8 * j : 8 * j + 8, :], axis=0, keepdims=True) for j in range(SHORT)
+        ] + [jnp.zeros((1, LANES), F32)]
         gathered = (
             lax.broadcasted_iota(jnp.int32, (LANES, LANES), 1)
             == at * PER + lax.broadcasted_iota(jnp.int32, (LANES, LANES), 0) // WIDTH
         ).astype(F32)
         part_out[share, 64:72, :] += jnp.dot(
-            jnp.concatenate(terms, axis=0), gathered,
+            jnp.concatenate(sums, axis=0), gathered,
             preferred_element_type=F32, precision=lax.Precision.HIGHEST,
         )
+
+    def second_half(q):
+        add_taps(lax.rem(q + chunks - 1, chunks))
+        earlier = jnp.maximum(q - 1, 0)
+        taps = taps_of(earlier)
+        lanes = chunk(q)
+        share, at, own_groups = place(q)
+        split_groups(
+            split,
+            (g_all[BLOCK:rows, lanes].astype(F32) * act_all[BLOCK:, lanes].astype(F32)).astype(BF16),
+        )
+        window = cot_all[BLOCK : 3 * BLOCK, lanes]
+        for part in range(PARTS):
+            for g in range(part * PER // PARTS, (part + 1) * PER // PARTS):
+                own = slice(g * BLOCK, (g + 1) * BLOCK)
+                ext = slice(g * EXT, (g + 1) * EXT)
+                circ = circ_all[q, own, :]
+                table[own, 0:LANES] = circ * win_mask[1, :, 0:LANES]
+                table[own, LANES:] = circ * win_mask[1, :, LANES:]
+                ext_table[ext, 0:LANES] = circ[0:EXT] * ext_mask[:, 0:LANES]
+                ext_table[ext, LANES:] = circ[0:EXT] * ext_mask[:, LANES:]
+            correlate(corr, split, cot_all, BLOCK, lanes, part)
+            own = slice(part * PER // PARTS * BLOCK, (part + 1) * PER // PARTS * BLOCK)
+            back_all[own, :] = jnp.dot(table[own, :], window, preferred_element_type=F32)
+            short_back(earlier, taps, part)
+        back_ext[...] = jnp.dot(
+            ext_table[...], cot_all[2 * BLOCK : 4 * BLOCK, lanes], preferred_element_type=F32
+        )
+        short_terms(earlier)
+        merge(merged, corr, diag_mask.at[1])
+        ag_s[0:BLOCK, :] = ag_all[:, lanes].astype(F32)
+        for part in range(PARTS):
+            own = slice(BLOCK + part * SUB, BLOCK + (part + 1) * SUB)
+            back = pick(back_all, part * SUB, SUB, BLOCK)
+            ag_s[own, :] = (back * g_all[own, lanes].astype(F32)).astype(BF16).astype(F32)
+            ggate_out[0, own, lanes] = (back * act_all[own, lanes].astype(F32)).astype(BF16)
+        back = pick(back_ext, 0, EXT, EXT)
+        ag_s[rows:, :] = (back * g_all[rows:, lanes].astype(F32)).astype(BF16).astype(F32)
 
     def one_piece(p, carry):
         piece(p).wait_recv()
@@ -302,6 +387,11 @@
         return lax.fori_loop(0, chunks // PIECES, inner, carry)
 
     lax.fori_loop(0, PIECES, one_piece, 0)
+    taps = taps_of(chunks - 1)
+    for part in range(PARTS):
+        short_back(chunks - 1, taps, part)
+    short_terms(chunks - 1)
+    add_taps(chunks - 1)
     for c in small:
         c.wait_send()
     gate_copy.wait_send()
@@ -342,8 +432,12 @@
             pltpu.VMEM((2, BLOCK, LANES), F32),
             pltpu.VMEM((SHORT - 1, rows, LANES), F32),
             pltpu.VMEM((SHORT - 1, rows, LANES), F32),
-            pltpu.VMEM((rows + EXT, LANES), F32),
+            pltpu.VMEM((rows + LANES, LANES), F32),
             pltpu.VMEM((rows + 8, LANES), F32),
+            pltpu.VMEM((BLOCK, LANES), F32),
+            pltpu.VMEM((BLOCK, LANES), F32),
+            pltpu.VMEM((8 * SHORT, LANES), F32),
+            pltpu.VMEM((PER * SUB, LANES), F32),
             pltpu.VMEM((rows + EXT, LANES), F32),
             pltpu.VMEM((stack, LANES), BF16),
             pltpu.VMEM((stack, 2 * LANES), BF16),

time: 104 us -> 93.6 us (0.90)
  Pallas kernels: 97.7 us -> 87 us
    pallas_call x1, Pallas kernels: 72 us -> 61.3 us  [layer_pair(): pl.pallas_call(pair_kernel, out_shape=(jax.ShapeDtypeStruct(inputs.shape,...]
where the time goes in v3:
time: 93.6 us; the launch traced here: 93.4 us
  Pallas kernels  87 us (93%)
  local copies, waits for them, and re-layouts  5.82 us (6%)
    pallas_call x1, Pallas kernels, layer_pair(): pl.pallas_call(pair_kernel, out_shape=(jax.ShapeDtypeStruct(inputs.shape,...  61.3 us
    pallas_call x1, Pallas kernels, reduce(): pl.pallas_call(functools.partial(reduce_kernel, scale), out_shape=(jax.Sh...  25.7 us
    unnamed x10, local copies, waits for them, and re-layouts  5.82 us

profile of v3, /device:TPU:16, one launch (start us, length us, event | category | flops | bytes accessed | tf_op | source)
XLA Modules:
  0.0 93.4 jit_solution(9339955218553063613)
XLA Ops:
  0.6 61.3 %layer_pair.1 = (bf16[1,256,4096]{2,1,0:T(8,128)(2,1)}, bf16[1,256,4096]{2,1,0:T(8,128)(2,1)}, f32[4,80,128]{2,1,0:T(8,128)}) custom-call(s32[1,64]{1,0:T(1,128)} %lengths.1, bf16[1,256,4096]{2,1,0:T(8,128)(2,1)} %inputs.1, bf16[1,256,4096]{2,1,0:T(8,128)(2,1)} %gates.1, bf16[1,256,4096]{2,1,0:T(8,128)(2,1)} %cot.1, bf16[7,64]{1,0:T(8,128)(2,1)} %short_ref.1, ...), custom_call_target="tpu_custom_call" | custom-call | tf_op jit(solution)/shard_map/layer_pair/pallas_call | solution.py:410
  61.9 25.7 %sum_terms.1 = (f32[7,64]{1,0:T(8,128)}, f32[64,128]{1,0:T(8,128)}) custom-call(f32[4,80,128]{2,1,0:T(8,128)} %get-tuple-element.11.part), custom_call_target="tpu_custom_call" | custom-call | tf_op jit(solution)/shard_map/sum_terms/pallas_call | solution.py:530
  87.6 0.0 copy-start
  87.6 3.3 %copy.14 = bf16[1,256,4096]{2,1,0:T(8,128)(2,1)} copy(bf16[1,256,4096]{2,1,0:T(8,128)(2,1)} %get-tuple-element.18) | data formatting | bytes 4194304
  90.9 0.0 copy-done
  90.9 0.0 copy-start.2
  90.9 0.0 copy-start.1
  90.9 1.3 %copy.15 = bf16[1,256,4096]{2,1,0:T(8,128)(2,1)} copy(bf16[1,256,4096]{2,1,0:T(8,128)(2,1)S(1)} %copy-done) | data formatting | bytes 4194304
  92.2 0.0 copy-done.2
  92.2 0.6 copy.16
  92.8 0.0 copy-done.1
  92.8 0.6 copy.17
Async XLA Ops:
  87.6 3.3 %copy-start = (bf16[1,256,4096]{2,1,0:T(8,128)(2,1)S(1)}, bf16[1,256,4096]{2,1,0:T(8,128)(2,1)}, u32[]{:S(2)}) copy-start(bf16[1,256,4096]{2,1,0:T(8,128)(2,1)} %get-tuple-element.19) | copy-start | bytes 6291460
  90.9 1.3 %copy-start.2 = (f32[7,64]{1,0:T(8,128)S(1)}, f32[7,64]{1,0:T(8,128)}, u32[]{:S(2)}) copy-start(f32[7,64]{1,0:T(8,128)} %get-tuple-element.20) | copy-start | bytes 5380
  90.9 1.9 %copy-start.1 = (f32[64,128]{1,0:T(8,128)S(1)}, f32[64,128]{1,0:T(8,128)}, u32[]{:S(2)}) copy-start(f32[64,128]{1,0:T(8,128)} %get-tuple-element.13) | copy-start | bytes 98308

commit v4 on v3

--- a/solution.py
+++ b/solution.py
@@ -410,9 +410,9 @@
     return pl.pallas_call(
         pair_kernel,
         out_shape=(
-            jax.ShapeDtypeStruct(inputs.shape, BF16),
-            jax.ShapeDtypeStruct(inputs.shape, BF16),
-            jax.ShapeDtypeStruct((shares, PART, LANES), F32),
+            pltpu.VMEM(inputs.shape, BF16),
+            pltpu.VMEM(inputs.shape, BF16),
+            pltpu.VMEM((shares, PART, LANES), F32),
         ),
         in_specs=[pl.BlockSpec(memory_space=pltpu.SMEM), anyspace, anyspace, anyspace, vmem, vmem],
         out_specs=(vmem, vmem, vmem),
@@ -543,7 +543,9 @@
             pltpu.SemaphoreType.DMA((5, 4)),
             pltpu.SemaphoreType.DMA((5, 4)),
         ],
-        compiler_params=pltpu.CompilerParams(collective_id=1, has_side_effects=True),
+        compiler_params=pltpu.CompilerParams(
+            collective_id=1, has_side_effects=True, vmem_limit_bytes=4 << 20
+        ),
         name="sum_terms",
     )(part)
 

time: 93.6 us -> 88.1 us (0.941)
  Pallas kernels: 87 us -> 83.4 us
  local copies, waits for them, and re-layouts: 5.82 us -> 3.85 us
    pallas_call x1, Pallas kernels: 61.3 us -> 59.2 us  [layer_pair(): pl.pallas_call(pair_kernel, out_shape=(pltpu.VMEM(inputs.shape, BF16), pl...]
    unnamed x10 -> x4, local copies, waits for them, and re-layouts: 5.82 us -> 3.85 us
    pallas_call x1, Pallas kernels: 25.7 us -> 24.2 us  [reduce(): pl.pallas_call(functools.partial(reduce_kernel, scale), out_shape=(jax.Sh...]
where the time goes in v4:
time: 88.1 us; the launch traced here: 87.9 us
  Pallas kernels  83.4 us (95%)
  local copies, waits for them, and re-layouts  3.85 us (4%)
    pallas_call x1, Pallas kernels, layer_pair(): pl.pallas_call(pair_kernel, out_shape=(pltpu.VMEM(inputs.shape, BF16), pl...  59.2 us
    pallas_call x1, Pallas kernels, reduce(): pl.pallas_call(functools.partial(reduce_kernel, scale), out_shape=(jax.Sh...  24.2 us
    unnamed x4, local copies, waits for them, and re-layouts  3.85 us

profile of v4, /device:TPU:16, one launch (start us, length us, event | category | flops | bytes accessed | tf_op | source)
XLA Modules:
  0.0 87.9 jit_solution(16757655494707922552)
XLA Ops:
  0.6 59.2 %layer_pair.1 = (bf16[1,256,4096]{2,1,0:T(8,128)(2,1)S(1)}, bf16[1,256,4096]{2,1,0:T(8,128)(2,1)S(1)}, f32[4,80,128]{2,1,0:T(8,128)S(1)}) custom-call(s32[1,64]{1,0:T(1,128)} %lengths.1, bf16[1,256,4096]{2,1,0:T(8,128)(2,1)} %inputs.1, bf16[1,256,4096]{2,1,0:T(8,128)(2,1)} %gates.1, bf16[1,256,4096]{2,1,0:T(8,128)(2,1)} %cot.1, bf16[7,64]{1,0:T(8,128)(2,1)} %short_ref.1, ...), custom_call_target="tpu_custom_call" | custom-call | tf_op jit(solution)/shard_map/layer_pair/pallas_call | solution.py:410
  59.8 24.2 %sum_terms.1 = (f32[7,64]{1,0:T(8,128)S(1)}, f32[64,128]{1,0:T(8,128)S(1)}) custom-call(f32[4,80,128]{2,1,0:T(8,128)S(1)} %get-tuple-element.11.part), custom_call_target="tpu_custom_call" | custom-call | tf_op jit(solution)/shard_map/sum_terms/pallas_call | solution.py:530
  84.1 1.3 %copy.14 = bf16[1,256,4096]{2,1,0:T(8,128)(2,1)} copy(bf16[1,256,4096]{2,1,0:T(8,128)(2,1)S(1)} %get-tuple-element.14) | data formatting | bytes 4194304
  85.4 1.3 %copy.15 = bf16[1,256,4096]{2,1,0:T(8,128)(2,1)} copy(bf16[1,256,4096]{2,1,0:T(8,128)(2,1)S(1)} %get-tuple-element.15) | data formatting | bytes 4194304
  86.7 0.6 copy.16
  87.3 0.6 copy.17

commit v5 on v4

--- a/solution.py
+++ b/solution.py
@@ -220,17 +220,16 @@
     )
     gate_copy.start()
     for p in range(PIECES):
-        piece(p).start()
+        piece(lax.rem(f * (PIECES // peers) + p, PIECES)).start()
 
     prepare(lengths, win_mask, ext_mask, diag_mask, fwd_mask, bwd_mask, rcol, row0)
     cot_all[rows + HALO :, :] = jnp.zeros((cot_all.shape[0] - rows - HALO, channels), BF16)
     part_out[...] = jnp.zeros_like(part_out)
-    filt[f] = mine[...]
-    for c in small:
-        c.wait_recv()
+    filt32[f] = mine[...].astype(F32)
+    small[-1].wait_recv()
     for c in local:
         c.wait()
-    filt32[...] = filt[...].astype(F32)
+    origin = f * per_share
 
     def place(q):
         share, at = q // per_share, lax.rem(q, per_share)
@@ -263,11 +262,12 @@
         part_out[share, own_groups, :] += line_up(merged)
 
     merged[...] = jnp.zeros_like(merged)
-    load_next(0)
+    load_next(origin)
     for part in range(PARTS):
-        forward(0, taps_of(0), part)
-
-    def first_half(q, carry):
+        forward(origin, taps_of(origin), part)
+
+    def first_half(step, carry):
+        q = lax.rem(origin + step, chunks)
         lanes = chunk(q)
         share, at, own_groups = place(q)
         long_rows = filt32[share, own_groups, :]
@@ -276,7 +276,7 @@
         act = act_next[...]
         act_s[...] = act
         split_groups(split, (gate * act).astype(BF16))
-        later = jnp.minimum(q + 1, chunks - 1)
+        later = lax.rem(q + 1, chunks)
         taps = taps_of(later)
         load_next(later)
         window = cot_all[0 : 2 * BLOCK, lanes]
@@ -302,7 +302,13 @@
             ggate_out[0, own, lanes] = (back * act_s[own, :]).astype(BF16)
         return carry
 
-    lax.fori_loop(0, chunks, first_half, 0)
+    lax.fori_loop(0, per_share - 1, first_half, 0)
+    for d in range(1, peers):
+        small[d - 1].wait_recv()
+    for d in range(1, peers):
+        share = ring("fsdp", d)
+        filt32[share] = filt[share].astype(F32)
+    lax.fori_loop(per_share - 1, chunks, first_half, 0)
     gate_copy.wait_recv()
 
     ag_s[...] = jnp.zeros_like(ag_s)
@@ -341,7 +347,7 @@
 
     def second_half(q):
         add_taps(lax.rem(q + chunks - 1, chunks))
-        earlier = jnp.maximum(q - 1, 0)
+        earlier = lax.rem(q + chunks - 1, chunks)
         taps = taps_of(earlier)
         lanes = chunk(q)
         share, at, own_groups = place(q)
@@ -377,7 +383,8 @@
         back = pick(back_ext, 0, EXT, EXT)
         ag_s[rows:, :] = (back * g_all[rows:, lanes].astype(F32)).astype(BF16).astype(F32)
 
-    def one_piece(p, carry):
+    def one_piece(step, carry):
+        p = lax.rem(f * (PIECES // peers) + step, PIECES)
         piece(p).wait_recv()
 
         def inner(i, c):
@@ -387,11 +394,12 @@
         return lax.fori_loop(0, chunks // PIECES, inner, carry)
 
     lax.fori_loop(0, PIECES, one_piece, 0)
-    taps = taps_of(chunks - 1)
+    last = lax.rem(origin + chunks - 1, chunks)
+    taps = taps_of(last)
     for part in range(PARTS):
-        short_back(chunks - 1, taps, part)
-    short_terms(chunks - 1)
-    add_taps(chunks - 1)
+        short_back(last, taps, part)
+    short_terms(last)
+    add_taps(last)
     for c in small:
         c.wait_send()
     gate_copy.wait_send()

time: 88.1 us -> 88.9 us (level)
  no operation moved by 1% of the time
where the time goes in v5:
time: 88.9 us; the launch traced here: 88.7 us
  Pallas kernels  84.2 us (95%)
  local copies, waits for them, and re-layouts  3.85 us (4%)
    pallas_call x1, Pallas kernels, layer_pair(): pl.pallas_call(pair_kernel, out_shape=(pltpu.VMEM(inputs.shape, BF16), pl...  60 us
    pallas_call x1, Pallas kernels, reduce(): pl.pallas_call(functools.partial(reduce_kernel, scale), out_shape=(jax.Sh...  24.2 us
    unnamed x4, local copies, waits for them, and re-layouts  3.85 us

profile of v5, /device:TPU:16, one launch (start us, length us, event | category | flops | bytes accessed | tf_op | source)
XLA Modules:
  0.0 88.7 jit_solution(8443963242665055260)
XLA Ops:
  0.6 60.0 %layer_pair.1 = (bf16[1,256,4096]{2,1,0:T(8,128)(2,1)S(1)}, bf16[1,256,4096]{2,1,0:T(8,128)(2,1)S(1)}, f32[4,80,128]{2,1,0:T(8,128)S(1)}) custom-call(s32[1,64]{1,0:T(1,128)} %lengths.1, bf16[1,256,4096]{2,1,0:T(8,128)(2,1)} %inputs.1, bf16[1,256,4096]{2,1,0:T(8,128)(2,1)} %gates.1, bf16[1,256,4096]{2,1,0:T(8,128)(2,1)} %cot.1, bf16[7,64]{1,0:T(8,128)(2,1)} %short_ref.1, ...), custom_call_target="tpu_custom_call" | custom-call | tf_op jit(solution)/shard_map/layer_pair/pallas_call | solution.py:418
  60.6 24.2 %sum_terms.1 = (f32[7,64]{1,0:T(8,128)S(1)}, f32[64,128]{1,0:T(8,128)S(1)}) custom-call(f32[4,80,128]{2,1,0:T(8,128)S(1)} %get-tuple-element.11.part), custom_call_target="tpu_custom_call" | custom-call | tf_op jit(solution)/shard_map/sum_terms/pallas_call | solution.py:538
  84.9 1.3 %copy.14 = bf16[1,256,4096]{2,1,0:T(8,128)(2,1)} copy(bf16[1,256,4096]{2,1,0:T(8,128)(2,1)S(1)} %get-tuple-element.14) | data formatting | bytes 4194304
  86.2 1.3 %copy.15 = bf16[1,256,4096]{2,1,0:T(8,128)(2,1)} copy(bf16[1,256,4096]{2,1,0:T(8,128)(2,1)S(1)} %get-tuple-element.15) | data formatting | bytes 4194304
  87.5 0.6 copy.16
  88.1 0.6 copy.17
